TPU v7x, 32 devices: a whole 2x2x4 slice. The times are simulated.
32 devices in a mesh: fsdp: 8 (over y, x, core), tp: 4 (over z).
Axes of the slice: x: 2, y: 2, z: 4, core: 2. Of those that a mesh axis runs over, the one named last changes fastest.
Arguments:
- x_in: bfloat16 [4096, 1600], P(('fsdp', 'tp')), may hold values from -6 to 6
- lengths: int32 [2], replicated, may hold values from 256 to 3840, as said below
- w_q: bfloat16 [2, 1600, 1600], P(None, 'fsdp'), may hold values from -0.15625 to 0.15625
- w_kv: bfloat16 [2, 1600, 640], P(None, 'fsdp'), may hold values from -0.15625 to 0.15625
- w_o: bfloat16 [2, 1600, 1600], P(None, 'fsdp'), may hold values from -0.15625 to 0.15625
- input_weight: bfloat16 [2, 1600, 3, 3200], P(None, 'fsdp', None, 'tp'), may hold values from -0.15625 to 0.15625
- a_log: float32 [2, 3200], P(None, 'tp'), may hold values from -7 to -2
- dt_bias: float32 [2, 3200], P(None, 'tp'), may hold values from -3 to 0
- d_skip: float32 [2, 3200], P(None, 'tp'), may hold values from 0.5 to 1.5
- w_bc: bfloat16 [2, 1600, 32], replicated, may hold values from -0.15625 to 0.15625
- w_out: bfloat16 [2, 3200, 1600], P(None, 'tp', 'fsdp'), may hold values from -0.109375 to 0.109375
- gains: float32 [2, 4, 1600], replicated, may hold values from 0.5 to 1.5
- gate_up_weight: bfloat16 [2, 1600, 2, 5504], P(None, 'fsdp', None, 'tp'), may hold values from -0.15625 to 0.15625
- w_down: bfloat16 [2, 5504, 1600], P(None, 'tp', 'fsdp'), may hold values from -0.078125 to 0.078125
- cotangent: bfloat16 [4096, 1600], P(('fsdp', 'tp')), may hold values from -6 to 6
Outputs:
- block_out: bfloat16 [4096, 1600], P(('fsdp', 'tp'))
- grad_input: float32 [4096, 1600], P(('fsdp', 'tp'))
- grad_w_q: float32 [2, 1600, 1600], P(None, 'fsdp')
- grad_w_kv: float32 [2, 1600, 640], P(None, 'fsdp')
- grad_w_o: float32 [2, 1600, 1600], P(None, 'fsdp')
- grad_w_in: float32 [2, 1600, 3, 3200], P(None, 'fsdp', None, 'tp')
- grad_a_log: float32 [2, 3200], P(None, 'fsdp')
- grad_dt_bias: float32 [2, 3200], P(None, 'fsdp')
- grad_d_skip: float32 [2, 3200], P(None, 'fsdp')
- grad_w_bc: float32 [2, 1600, 32], P(None, 'fsdp')
- grad_w_out: float32 [2, 3200, 1600], P(None, 'tp', 'fsdp')
- grad_gains: float32 [2, 4, 1600], P(None, None, 'fsdp')
- grad_w_gu: float32 [2, 1600, 2, 5504], P(None, 'fsdp', None, 'tp')
- grad_w_down: float32 [2, 5504, 1600], P(None, 'tp', 'fsdp')
Inputs may be any that keep to these rules, and one draw needn't show every extreme that they name: The 2 lengths sum to 4096; both 256 and 3840 occur in every draw.
All inputs are finite; a program needn't handle non-finite values.
Results may differ from a plain program's by a relative error of at most 0.033.
Values may be sent and summed in bfloat16 or wider, within the bound.
No kernel may reach another device: no remote copies, remote signals or barrier semaphores. Data moves between devices by JAX's collectives and lax.ppermute only.
A program may use at most 512 MiB of HBM per device.

v0:
```python
import math

import jax
import jax.numpy as jnp
from jax import lax
from jax.sharding import PartitionSpec as P

HEADS = 25
HEAD = 64
KV_HEADS = 5
WINDOW = 1024


EPSILON = 1e-05
TOP_PRECISION = lax.Precision.HIGHEST


def shifted(value, axis, steps):
    count = lax.axis_size(axis)
    leading, last = (max(0, -steps), min(count, count - steps))
    return lax.ppermute(value, axis, [(source, source + steps) for source in range(leading, last)])


def carried_in(value, axis, combine, identity):
    count, place = (lax.axis_size(axis), lax.axis_index(axis))
    everything = jax.tree.map(
        lambda part, kind: lax.all_gather(part.astype(kind), axis),
        value,
        (jnp.bfloat16, jnp.bfloat16),
    )
    start = jax.tree.map(
        lambda part, zero: jnp.broadcast_to(jnp.asarray(zero, part.dtype), part.shape),
        value,
        identity,
    )

    def lap(k, before):
        reached = k < place
        new = combine(
            before, jax.tree.map(lambda part, own: part[k].astype(own.dtype), everything, value)
        )
        return jax.tree.map(lambda a, b: jnp.where(reached, a, b), new, before)

    return lax.fori_loop(0, count, lap, start)


def carried_in_2(value, axis, join, neutral):
    count = lax.axis_size(axis)
    place = lax.axis_index(axis)
    ahead = count - 1 - place
    gathered = jax.tree.map(
        lambda a, kind: lax.all_gather(a.astype(kind), axis),
        value,
        jax.tree.map(lambda a: jnp.bfloat16 if a.dtype == jnp.float32 else a.dtype, value),
    )
    state = jax.tree.map(lambda a, e: jnp.zeros_like(a) + jnp.asarray(e, a.dtype), value, neutral)

    def one(lap, state):
        source = count - 1 - lap
        return join(
            state,
            jax.tree.map(
                lambda a, own: lax.dynamic_index_in_dim(a, source, 0, False).astype(own.dtype),
                gathered,
                value,
            ),
        )

    return lax.fori_loop(0, ahead, one, state)


def rms_scale(values, gain_row):
    return (
        values * lax.rsqrt(jnp.mean(values * values, axis=-1, keepdims=True) + EPSILON) * gain_row
    )


def branch_mix(attn_out, mamba_out, gain_attn, gain_mamba):
    return 0.5 * (rms_scale(attn_out, gain_attn) + rms_scale(mamba_out, gain_mamba))


def mamba_gate(scanned, inflow_u, gate_z, skip_row):
    return (scanned + skip_row * inflow_u) * jax.nn.silu(gate_z)


def swiglu(gate_up_product):
    return jax.nn.silu(gate_up_product[:, 0]) * gate_up_product[:, 1]


def sequence_ids(lengths, places):
    seq_ends = jnp.cumsum(lengths)
    starts = seq_ends - lengths
    numbers = jnp.sum((places[:, None] >= starts[None, :]).astype(jnp.int32), axis=1) - 1
    return numbers


def window_scores(query_four, keys_all, allowed):
    raw_scores = (
        jnp.einsum("tkgd,skd->kgts", query_four, keys_all, preferred_element_type=jnp.float32)
        * 0.125
    )
    return jnp.where(allowed, raw_scores, -1e30)


def chain_combine(earlier, later):
    return (earlier[0] * later[0], later[0][:, None] * earlier[1] + later[1])


def scan_parts(inflow_u, pre_steps, b_rows, c_rows, a_row, bias_row, numbers, prev_number):
    row_count, channels = inflow_u.shape
    block_len = math.gcd(row_count, 64)
    blocks = row_count // block_len
    step_sizes = jax.nn.softplus(pre_steps + bias_row)
    rate = -jnp.exp(a_row)
    lower_tri = jnp.arange(block_len)[:, None] >= jnp.arange(block_len)[None, :]
    running = jnp.einsum(
        "ts,bsc->btc",
        lower_tri.astype(jnp.float32),
        (step_sizes * rate).reshape(blocks, block_len, channels),
        precision=TOP_PRECISION,
    )
    totals = running[:, -1, :]
    cum_all = (running + (jnp.cumsum(totals, axis=0) - totals)[:, None, :]).reshape(
        row_count, channels
    )
    inflow = (step_sizes * inflow_u).reshape(blocks, block_len, channels)
    id_blocks = numbers.reshape(blocks, block_len)
    befores = jnp.concatenate([jnp.reshape(prev_number, (1,)), id_blocks[:-1, -1]])

    def block_step(carry_state, row_slices):
        run_b, in_b, b_b, c_b, id_b, before = row_slices
        same_seq = lower_tri & (id_b[:, None] == id_b[None, :])
        gap_b = run_b[:, None, :] - run_b[None, :, :]
        decay_pairs = jnp.exp(jnp.where(same_seq[:, :, None], gap_b, -1e30))
        inner_bc = jnp.dot(c_b, b_b.T, precision=TOP_PRECISION)
        within = jnp.sum(decay_pairs * inner_bc[:, :, None] * in_b[None, :, :], axis=1)
        alive_rows = (id_b == before).astype(jnp.float32)
        from_state = (
            jnp.exp(run_b)
            * alive_rows[:, None]
            * jnp.dot(c_b, carry_state.T, precision=TOP_PRECISION)
        )
        tail_decay = (
            jnp.exp(run_b[-1][None, :] - run_b) * (id_b == id_b[-1]).astype(jnp.float32)[:, None]
        )
        carry_state = (jnp.exp(run_b[-1]) * alive_rows[-1])[:, None] * carry_state + jnp.dot(
            (tail_decay * in_b).T, b_b, precision=TOP_PRECISION
        )
        return (carry_state, within + from_state)

    start_state = jnp.zeros((channels, b_rows.shape[1]), jnp.float32)
    row_slices = (
        running,
        inflow,
        b_rows.reshape(blocks, block_len, -1),
        c_rows.reshape(blocks, block_len, -1),
        id_blocks,
        befores,
    )
    end_state, outputs = lax.scan(jax.checkpoint(block_step), start_state, row_slices)
    alive_all = (numbers == prev_number).astype(jnp.float32)
    carry_decay = jnp.exp(cum_all[-1]) * alive_all[-1]
    return (outputs.reshape(row_count, channels), carry_decay, end_state, cum_all, alive_all)


def carry_term(cum_all, alive_all, c_rows, carried):
    return (
        jnp.exp(cum_all) * alive_all[:, None] * jnp.dot(c_rows, carried.T, precision=TOP_PRECISION)
    )


def scan_whole(inflow_u, pre_steps, b_rows, c_rows, a_row, bias_row, carried, numbers, prev_number):
    local_y, carry_decay, end_state, cum_all, alive_all = scan_parts(
        inflow_u, pre_steps, b_rows, c_rows, a_row, bias_row, numbers, prev_number
    )
    return (local_y + carry_term(cum_all, alive_all, c_rows, carried), carry_decay, end_state)


def fetch_weights(w_q, w_kv, w_o, input_weight, w_out, gate_up_weight, w_down, layer_index):
    return (
        lax.all_gather(w_q[layer_index], "fsdp", axis=0, tiled=True),
        lax.all_gather(w_kv[layer_index], "fsdp", axis=0, tiled=True),
        lax.all_gather(w_o[layer_index], "fsdp", axis=0, tiled=True),
        lax.all_gather(input_weight[layer_index], "fsdp", axis=0, tiled=True),
        lax.all_gather(w_out[layer_index], "fsdp", axis=1, tiled=True),
        lax.all_gather(gate_up_weight[layer_index], "fsdp", axis=0, tiled=True),
        lax.all_gather(w_down[layer_index], "fsdp", axis=1, tiled=True),
    )


def fetch_again(w_q, w_kv, w_o, input_weight, w_out, gate_up_weight, w_down, layer_index):
    return (
        lax.all_gather(w_q[layer_index], "fsdp", axis=0, tiled=True),
        lax.all_gather(w_kv[layer_index], "fsdp", axis=0, tiled=True),
        lax.all_gather(w_o[layer_index], "fsdp", axis=0, tiled=True),
        lax.all_gather(input_weight[layer_index], "fsdp", axis=0, tiled=True),
        lax.all_gather(w_out[layer_index], "fsdp", axis=1, tiled=True),
        lax.all_gather(gate_up_weight[layer_index], "fsdp", axis=0, tiled=True),
        lax.all_gather(w_down[layer_index], "fsdp", axis=1, tiled=True),
    )


def reduce_rows(values):
    return lax.psum_scatter(
        values.astype(jnp.bfloat16), "tp", scatter_dimension=0, tiled=True
    ).astype(jnp.float32)


def spread_rows(values):
    return lax.all_gather(values, "tp", axis=0, tiled=True)


def reduce_grads(local_terms):
    shards = (
        lax.psum_scatter(
            local_terms[0].astype(jnp.bfloat16), "fsdp", scatter_dimension=1, tiled=True
        ).astype(jnp.float32),
        lax.psum_scatter(
            local_terms[1].astype(jnp.bfloat16), "fsdp", scatter_dimension=1, tiled=True
        ).astype(jnp.float32),
        lax.psum_scatter(
            local_terms[2].astype(jnp.bfloat16), "fsdp", scatter_dimension=1, tiled=True
        ).astype(jnp.float32),
        lax.psum_scatter(
            local_terms[3].astype(jnp.bfloat16), "fsdp", scatter_dimension=1, tiled=True
        ).astype(jnp.float32),
        lax.psum_scatter(
            local_terms[4].astype(jnp.bfloat16), "fsdp", scatter_dimension=2, tiled=True
        ).astype(jnp.float32),
        lax.psum_scatter(
            local_terms[5].astype(jnp.bfloat16), "fsdp", scatter_dimension=1, tiled=True
        ).astype(jnp.float32),
        lax.psum_scatter(
            local_terms[6].astype(jnp.bfloat16), "fsdp", scatter_dimension=2, tiled=True
        ).astype(jnp.float32),
        lax.psum_scatter(
            local_terms[7].astype(jnp.bfloat16), "fsdp", scatter_dimension=2, tiled=True
        ).astype(jnp.float32),
        lax.psum_scatter(
            local_terms[8].astype(jnp.bfloat16), "fsdp", scatter_dimension=1, tiled=True
        ).astype(jnp.float32),
        lax.psum_scatter(
            local_terms[9].astype(jnp.bfloat16), "fsdp", scatter_dimension=2, tiled=True
        ).astype(jnp.float32),
    )
    shared = (
        lax.psum(shards[0].astype(jnp.bfloat16), "tp").astype(jnp.float32),
        lax.psum(shards[1].astype(jnp.bfloat16), "tp").astype(jnp.float32),
        lax.psum(shards[2].astype(jnp.bfloat16), "tp").astype(jnp.float32),
        lax.psum(shards[7].astype(jnp.bfloat16), "tp").astype(jnp.float32),
        lax.psum(shards[8].astype(jnp.bfloat16), "tp").astype(jnp.float32),
        lax.psum(shards[9].astype(jnp.bfloat16), "tp").astype(jnp.float32),
    )
    return (
        shared[0],
        shared[1],
        shared[2],
        shards[3],
        shared[5][:, 0],
        shared[5][:, 1],
        shared[5][:, 2],
        shared[4],
        shards[4],
        shared[3],
        shards[5],
        shards[6],
    )


def body(
    x_in,
    lengths,
    w_q,
    w_kv,
    w_o,
    input_weight,
    a_log,
    dt_bias,
    d_skip,
    w_bc,
    w_out,
    gains,
    gate_up_weight,
    w_down,
    cotangent,
):
    rows_own = x_in.shape[0]
    tp_count = lax.axis_size("tp")
    group_rows = rows_own * tp_count
    fsdp_index = lax.axis_index("fsdp")
    tp_index = lax.axis_index("tp")
    hop_total = -(-WINDOW // group_rows)
    layers = w_q.shape[0]
    half_kv = w_kv.shape[2] // 2
    heads_per = HEADS // KV_HEADS
    chan_count = a_log.shape[1]
    group_places = fsdp_index * group_rows + jnp.arange(group_rows, dtype=jnp.int32)
    own_places = lax.dynamic_slice_in_dim(group_places, tp_index * rows_own, rows_own, 0)
    key_places = (fsdp_index - hop_total) * group_rows + jnp.arange(
        (hop_total + 1) * group_rows, dtype=jnp.int32
    )
    group_numbers = sequence_ids(lengths, group_places)
    own_numbers = sequence_ids(lengths, own_places)
    key_numbers = sequence_ids(lengths, key_places)
    prev_number = sequence_ids(lengths, group_places[:1] - 1)[0]
    relative = own_places[:, None] - key_places[None, :]
    allowed = (relative >= 0) & (relative < WINDOW) & (own_numbers[:, None] == key_numbers[None, :])

    def forward_layer(stream, weights, layer_index):
        (
            full_q,
            full_kv,
            full_o,
            complete_input_weight,
            full_out,
            complete_gate_up_weight,
            full_down,
        ) = weights
        layer_gains = gains[layer_index]
        normalized_rows = rms_scale(stream, layer_gains[0]).astype(jnp.bfloat16)
        query_rows = jnp.dot(normalized_rows, full_q, preferred_element_type=jnp.float32).astype(
            jnp.bfloat16
        )
        key_value = jnp.dot(normalized_rows, full_kv, preferred_element_type=jnp.float32).astype(
            jnp.bfloat16
        )
        normalized_rows_full, kv_all = (
            lax.all_gather(normalized_rows, "tp", axis=0, tiled=True),
            lax.all_gather(key_value, "tp", axis=0, tiled=True),
        )
        pieces = []
        for hop_count in range(hop_total, 0, -1):
            pieces.append(shifted(kv_all, "fsdp", hop_count))
        kv_window = jnp.concatenate(pieces + [kv_all], axis=0)
        keys_all = kv_window[:, :half_kv].reshape(-1, KV_HEADS, HEAD)
        values_all = kv_window[:, half_kv:].reshape(-1, KV_HEADS, HEAD)
        query_four = query_rows.reshape(rows_own, KV_HEADS, heads_per, HEAD)
        scores = window_scores(query_four, keys_all, allowed)
        row_top = jnp.max(scores, axis=-1, keepdims=True)
        log_total = row_top + jnp.log(jnp.sum(jnp.exp(scores - row_top), axis=-1, keepdims=True))
        soft_probs = jnp.exp(scores - log_total).astype(jnp.bfloat16)
        attended = (
            jnp.einsum("kgts,skd->tkgd", soft_probs, values_all, preferred_element_type=jnp.float32)
            .reshape(rows_own, -1)
            .astype(jnp.bfloat16)
        )
        attn_out = jnp.dot(attended, full_o, preferred_element_type=jnp.float32)
        projected_rows = jnp.einsum(
            "pu,usw->psw",
            normalized_rows_full,
            complete_input_weight,
            preferred_element_type=jnp.float32,
        )
        inflow_u = projected_rows[:, 0]
        gate_z = projected_rows[:, 1]
        pre_steps = projected_rows[:, 2]
        bc_rows = jnp.dot(
            normalized_rows_full, w_bc[layer_index], preferred_element_type=jnp.float32
        )
        state_count = bc_rows.shape[1] // 2
        b_rows = bc_rows[:, :state_count]
        c_rows = bc_rows[:, state_count:]
        local_y, carry_decay, end_state, cum_all, alive_all = scan_parts(
            inflow_u,
            pre_steps,
            b_rows,
            c_rows,
            a_log[layer_index],
            dt_bias[layer_index],
            group_numbers,
            prev_number,
        )
        identity = (jnp.ones_like(carry_decay), jnp.zeros_like(end_state))
        _, carried = carried_in((carry_decay, end_state), "fsdp", chain_combine, identity)
        scanned = local_y + carry_term(cum_all, alive_all, c_rows, carried)
        mamba_mid = mamba_gate(scanned, inflow_u, gate_z, d_skip[layer_index]).astype(jnp.bfloat16)
        mamba_out = reduce_rows(jnp.dot(mamba_mid, full_out, preferred_element_type=jnp.float32))
        middle = stream + branch_mix(attn_out, mamba_out, layer_gains[1], layer_gains[2])
        feedforward_input = rms_scale(middle, layer_gains[3]).astype(jnp.bfloat16)
        feedforward_input_full = lax.all_gather(feedforward_input, "tp", axis=0, tiled=True)
        gate_up_product = jnp.einsum(
            "pu,usw->psw",
            feedforward_input_full,
            complete_gate_up_weight,
            preferred_element_type=jnp.float32,
        )
        hidden = swiglu(gate_up_product).astype(jnp.bfloat16)
        ffn_out = reduce_rows(jnp.dot(hidden, full_down, preferred_element_type=jnp.float32))
        retained_values = {
            "stream": stream,
            "normed": normalized_rows,
            "query_four": query_four,
            "keys_all": keys_all,
            "values_all": values_all,
            "log_total": log_total,
            "attended": attended,
            "attn_out": attn_out,
            "normed_all": normalized_rows_full,
            "inflow_u": inflow_u,
            "gate_z": gate_z,
            "pre_steps": pre_steps,
            "b_rows": b_rows,
            "c_rows": c_rows,
            "cum_all": cum_all,
            "alive_all": alive_all,
            "carry_decay": carry_decay,
            "carried": carried,
            "scanned": scanned,
            "mamba_mid": mamba_mid,
            "mamba_out": mamba_out,
            "middle": middle,
            "ffn_all": feedforward_input_full,
            "gate_up": gate_up_product,
            "hidden": hidden,
        }
        return (middle + ffn_out, retained_values)

    def backward_layer(grad_out, weights, retained_values, layer_index):
        (
            full_q,
            full_kv,
            full_o,
            complete_input_weight,
            full_out,
            complete_gate_up_weight,
            full_down,
        ) = weights
        layer_gains = gains[layer_index]
        grad_ffn_all = spread_rows(grad_out.astype(jnp.bfloat16))
        grad_hidden = jnp.dot(grad_ffn_all, full_down.T, preferred_element_type=jnp.float32)
        grad_down = jnp.dot(
            retained_values["hidden"].T, grad_ffn_all, preferred_element_type=jnp.float32
        )
        _, swiglu_pull = jax.vjp(swiglu, retained_values["gate_up"])
        gradient_gate_up_product = swiglu_pull(grad_hidden)[0].astype(jnp.bfloat16)
        grad_gu = jnp.einsum(
            "zy,zmj->ymj",
            retained_values["ffn_all"],
            gradient_gate_up_product,
            preferred_element_type=jnp.float32,
        )
        grad_ffn_in = jnp.einsum(
            "bqs,fqs->bf",
            gradient_gate_up_product,
            complete_gate_up_weight,
            preferred_element_type=jnp.float32,
        )
        grad_ffn_own = lax.psum_scatter(
            grad_ffn_in.astype(jnp.bfloat16), "tp", scatter_dimension=0, tiled=True
        ).astype(jnp.float32)
        _, norm_pull = jax.vjp(rms_scale, retained_values["middle"], layer_gains[3])
        grad_mid_norm, grad_gain_ffn = norm_pull(grad_ffn_own)
        grad_middle = grad_out + grad_mid_norm
        _, mix_pull = jax.vjp(
            branch_mix,
            retained_values["attn_out"],
            retained_values["mamba_out"],
            layer_gains[1],
            layer_gains[2],
        )
        grad_attn_out, grad_mamba_out, grad_gain_attn, grad_gain_mamba = mix_pull(grad_middle)
        grad_mamba_all = spread_rows(grad_mamba_out.astype(jnp.bfloat16))
        grad_mid = jnp.dot(grad_mamba_all, full_out.T, preferred_element_type=jnp.float32)
        grad_wout = jnp.dot(
            retained_values["mamba_mid"].T, grad_mamba_all, preferred_element_type=jnp.float32
        )
        _, gate_pull = jax.vjp(
            mamba_gate,
            retained_values["scanned"],
            retained_values["inflow_u"],
            retained_values["gate_z"],
            d_skip[layer_index],
        )
        grad_scanned, grad_inflow, grad_gate_z, grad_skip = gate_pull(grad_mid)
        carried = retained_values["carried"]
        decay_rows = jnp.exp(retained_values["cum_all"]) * retained_values["alive_all"][:, None]
        grad_carried = jnp.dot(
            (decay_rows * grad_scanned).T, retained_values["c_rows"], precision=TOP_PRECISION
        )
        identity = (jnp.ones_like(retained_values["carry_decay"]), jnp.zeros_like(grad_carried))
        _, back_chain = carried_in_2(
            (retained_values["carry_decay"], grad_carried), "fsdp", chain_combine, identity
        )
        grad_decay = jnp.sum(back_chain * carried, axis=1)

        def whole_scan(inflow_u, pre_steps, b_rows, c_rows, a_row, bias_row):
            return scan_whole(
                inflow_u,
                pre_steps,
                b_rows,
                c_rows,
                a_row,
                bias_row,
                carried,
                group_numbers,
                prev_number,
            )

        _, whole_pull = jax.vjp(
            whole_scan,
            retained_values["inflow_u"],
            retained_values["pre_steps"],
            retained_values["b_rows"],
            retained_values["c_rows"],
            a_log[layer_index],
            dt_bias[layer_index],
        )
        grad_u_scan, grad_pre, grad_b_rows, grad_c_rows, grad_alog, grad_bias = whole_pull(
            (grad_scanned, grad_decay, back_chain)
        )
        gradient_projected_rows = jnp.stack(
            [grad_inflow + grad_u_scan, grad_gate_z, grad_pre], axis=1
        ).astype(jnp.bfloat16)
        grad_win = jnp.einsum(
            "zy,zmj->ymj",
            retained_values["normed_all"],
            gradient_projected_rows,
            preferred_element_type=jnp.float32,
        )
        grad_bc = jnp.concatenate([grad_b_rows, grad_c_rows], axis=1)
        bc_weight = w_bc[layer_index].astype(jnp.float32)
        grad_normed_all = jnp.einsum(
            "bqs,fqs->bf",
            gradient_projected_rows,
            complete_input_weight,
            preferred_element_type=jnp.float32,
        ) + jnp.dot(grad_bc, bc_weight.T, precision=TOP_PRECISION)
        grad_wbc = jnp.dot(
            retained_values["normed_all"].T,
            grad_bc,
            precision=TOP_PRECISION,
            preferred_element_type=jnp.float32,
        )
        attn_grad_low = grad_attn_out.astype(jnp.bfloat16)
        grad_wo = jnp.dot(
            retained_values["attended"].T, attn_grad_low, preferred_element_type=jnp.float32
        )
        grad_attended = jnp.dot(attn_grad_low, full_o.T, preferred_element_type=jnp.float32).astype(
            jnp.bfloat16
        )
        grad_four = grad_attended.reshape(rows_own, KV_HEADS, heads_per, HEAD)
        query_four = retained_values["query_four"]
        keys_all = retained_values["keys_all"]
        values_all = retained_values["values_all"]
        soft_probs = jnp.exp(
            window_scores(query_four, keys_all, allowed) - retained_values["log_total"]
        )
        grad_soft = jnp.einsum(
            "tkgd,skd->kgts", grad_four, values_all, preferred_element_type=jnp.float32
        )
        row_delta = jnp.sum(soft_probs * grad_soft, axis=-1, keepdims=True)
        grad_scores = (soft_probs * (grad_soft - row_delta)).astype(jnp.bfloat16)
        grad_query = (
            (
                jnp.einsum(
                    "kgts,skd->tkgd", grad_scores, keys_all, preferred_element_type=jnp.float32
                )
                * 0.125
            )
            .reshape(rows_own, -1)
            .astype(jnp.bfloat16)
        )
        grad_keys = (
            jnp.einsum(
                "kgts,tkgd->skd", grad_scores, query_four, preferred_element_type=jnp.float32
            )
            * 0.125
        )
        grad_values = jnp.einsum(
            "kgts,tkgd->skd",
            soft_probs.astype(jnp.bfloat16),
            grad_four,
            preferred_element_type=jnp.float32,
        )
        grad_window = jnp.concatenate(
            [grad_keys.reshape(-1, half_kv), grad_values.reshape(-1, half_kv)], axis=1
        )
        grad_kv_group = grad_window[hop_total * group_rows :]
        for hop_count in range(1, hop_total + 1):
            row_start = (hop_total - hop_count) * group_rows
            grad_kv_group = grad_kv_group + shifted(
                grad_window[row_start : row_start + group_rows].astype(jnp.bfloat16),
                "fsdp",
                -hop_count,
            ).astype(jnp.float32)
        grad_normed_own, grad_kv_own = (
            lax.psum_scatter(
                grad_normed_all.astype(jnp.bfloat16), "tp", scatter_dimension=0, tiled=True
            ).astype(jnp.float32),
            lax.psum_scatter(
                grad_kv_group.astype(jnp.bfloat16), "tp", scatter_dimension=0, tiled=True
            ).astype(jnp.float32),
        )
        grad_kv_low = grad_kv_own.astype(jnp.bfloat16)
        grad_wq = jnp.dot(
            retained_values["normed"].T, grad_query, preferred_element_type=jnp.float32
        )
        grad_wkv = jnp.dot(
            retained_values["normed"].T, grad_kv_low, preferred_element_type=jnp.float32
        )
        grad_normed = (
            grad_normed_own
            + jnp.dot(grad_query, full_q.T, preferred_element_type=jnp.float32)
            + jnp.dot(grad_kv_low, full_kv.T, preferred_element_type=jnp.float32)
        )
        _, in_pull = jax.vjp(rms_scale, retained_values["stream"], layer_gains[0])
        grad_stream_norm, grad_gain_in = in_pull(grad_normed)
        grad_stream = grad_middle + grad_stream_norm
        grad_gains = jnp.stack([grad_gain_in, grad_gain_attn, grad_gain_mamba, grad_gain_ffn])
        ssm_local = jnp.stack([grad_alog, grad_bias, grad_skip])
        ssm_full = lax.dynamic_update_slice_in_dim(
            jnp.zeros((3, chan_count * tp_count), jnp.float32), ssm_local, tp_index * chan_count, 1
        )
        return (
            grad_stream,
            (
                grad_wq,
                grad_wkv,
                grad_wo,
                grad_win,
                grad_wout,
                grad_gu,
                grad_down,
                grad_gains,
                grad_wbc,
                ssm_full,
            ),
        )

    stream = x_in.astype(jnp.float32)
    saved_layers = []
    stored_weights = []
    for layer_index in range(layers):
        weights = fetch_weights(
            w_q, w_kv, w_o, input_weight, w_out, gate_up_weight, w_down, layer_index
        )
        stored_weights.append(None)
        stream, retained_values = forward_layer(stream, weights, layer_index)
        saved_layers.append(retained_values)
    block_out = stream.astype(jnp.bfloat16)
    grad_stream = cotangent.astype(jnp.float32)
    collected = []
    for layer_index in range(layers - 1, -1, -1):
        weights = fetch_again(
            w_q, w_kv, w_o, input_weight, w_out, gate_up_weight, w_down, layer_index
        )
        grad_stream, local_terms = backward_layer(
            grad_stream, weights, saved_layers[layer_index], layer_index
        )
        collected.insert(0, reduce_grads(tuple((member[None] for member in local_terms))))
    stacked = [
        jnp.concatenate([collected[layer_index][member] for layer_index in range(layers)], axis=0)
        for member in range(12)
    ]
    return (
        block_out,
        grad_stream,
        stacked[0],
        stacked[1],
        stacked[2],
        stacked[3],
        stacked[4],
        stacked[5],
        stacked[6],
        stacked[7],
        stacked[8],
        stacked[9],
        stacked[10],
        stacked[11],
    )


def solution(mesh):
    placed = (
        P(("fsdp", "tp"), None),
        P(),
        P(None, "fsdp", None),
        P(None, "fsdp", None),
        P(None, "fsdp", None),
        P(None, "fsdp", None, "tp"),
        P(None, "tp"),
        P(None, "tp"),
        P(None, "tp"),
        P(),
        P(None, "tp", "fsdp"),
        P(),
        P(None, "fsdp", None, "tp"),
        P(None, "tp", "fsdp"),
        P(("fsdp", "tp"), None),
    )
    return jax.shard_map(
        body,
        mesh=mesh,
        in_specs=placed,
        out_specs=(
            P(("fsdp", "tp"), None),
            P(("fsdp", "tp"), None),
            P(None, "fsdp", None),
            P(None, "fsdp", None),
            P(None, "fsdp", None),
            P(None, "fsdp", None, "tp"),
            P(None, "fsdp"),
            P(None, "fsdp"),
            P(None, "fsdp"),
            P(None, "fsdp", None),
            P(None, "tp", "fsdp"),
            P(None, None, "fsdp"),
            P(None, "fsdp", None, "tp"),
            P(None, "tp", "fsdp"),
        ),
        check_vma=False,
    )
```

profile of v0, /device:TPU:0, one launch (start us, length us, event | category | flops | bytes accessed | tf_op | source)
XLA Modules:
  0.0 2951.3 jit_solution(14272584155779051540)
XLA Ops:
  25.4 30.2 %all-gather.47.cloned.1.call-done = bf16[512,1600]{0,1:T(8,128)(2,1)} async-done(((bf16[128,1600]{0,1:T(8,128)(2,1)}), bf16[512,1600]{0,1:T(8,128)(2,1)}) %all-gather.47.cloned.1.call-update) | async-done | bytes 1638416 | tf_op jit(solution)/shard_map/all_gather | solution.py:328
  57.8 52.2 %all-gather.69.cloned.1.call-done = bf16[1,1600,3,800]{3,1,2,0:T(8,128)(2,1)} async-done(((bf16[1,200,3,800]{3,1,2,0:T(8,128)(2,1)}), bf16[1,1600,3,800]{3,1,2,0:T(8,128)(2,1)}) %all-gather.69.cloned.1.call-update) | async-done | bytes 7680016 | tf_op jit(solution)/shard_map/all_gather | solution.py:184
  126.4 98.7 %while.158 = (s32[]{:T(128)}, f32[800,16]{0,1:T(8,128)S(1)}, f32[8,64,800]{2,1,0:T(8,128)}, f32[8,64,800]{2,1,0:T(8,128)S(1)}, s32[8,64]{1,0:T(8,128)S(1)}, /*in...) while((s32[]{:T(128)}, f32[800,16]{0,1:T(8,128)S(1)}, ...), condition=%wide.region_11.12_spmd.clone, body=%wide.region_9.11_spmd.clone.sunk | while | flops 37151780 | bytes 2847946 | solution.py:160
  269.7 26.2 all_gather.123
  370.3 41.0 %all-gather.49.cloned.1.call-done = bf16[512,1600]{0,1:T(8,128)(2,1)} async-done(((bf16[128,1600]{0,1:T(8,128)(2,1)}), bf16[512,1600]{0,1:T(8,128)(2,1)}) %all-gather.49.cloned.1.call-update) | async-done | bytes 1638416 | tf_op jit(solution)/shard_map/all_gather | solution.py:380
  424.5 25.3 all-gather.75.cloned.1.call-done
  458.2 36.9 %reduce-scatter.85.cloned.1.call-done = bf16[128,1600]{1,0:T(8,128)(2,1)} async-done(((bf16[512,1600]{1,0:T(8,128)(2,1)}), bf16[128,1600]{1,0:T(8,128)(2,1)}) %reduce-scatter.85.cloned.1.call-update) | async-done | bytes 409616
  500.1 51.1 %all-gather.83.cloned.1.call-done = bf16[1,1600,3,800]{3,1,2,0:T(8,128)(2,1)} async-done(((bf16[1,200,3,800]{3,1,2,0:T(8,128)(2,1)}), bf16[1,1600,3,800]{3,1,2,0:T(8,128)(2,1)}) %all-gather.83.cloned.1.call-update) | async-done | bytes 7680016 | tf_op jit(solution)/shard_map/all_gather | solution.py:184
  551.2 40.4 %all-gather.51.cloned.1.call-done = bf16[512,1600]{0,1:T(8,128)(2,1)} async-done(((bf16[128,1600]{0,1:T(8,128)(2,1)}), bf16[512,1600]{0,1:T(8,128)(2,1)}) %all-gather.51.cloned.1.call-update) | async-done | bytes 1638416 | tf_op jit(solution)/shard_map/all_gather | solution.py:328
  610.5 110.0 %while.160 = (s32[]{:T(128)}, f32[800,16]{0,1:T(8,128)S(1)}, f32[8,64,800]{2,1,0:T(8,128)}, f32[8,64,800]{2,1,0:T(8,128)S(1)}, s32[8,64]{1,0:T(8,128)S(1)}, /*in...) while((s32[]{:T(128)}, f32[800,16]{0,1:T(8,128)S(1)}, ...), condition=%wide.region_25.26_spmd.clone, body=%wide.region_23.25_spmd.clone.sunk | while | flops 37151780 | bytes 2792394 | solution.py:160
  762.3 25.9 all_gather.136
  863.0 40.8 %all-gather.53.cloned.1.call-done = bf16[512,1600]{0,1:T(8,128)(2,1)} async-done(((bf16[128,1600]{0,1:T(8,128)(2,1)}), bf16[512,1600]{0,1:T(8,128)(2,1)}) %all-gather.53.cloned.1.call-update) | async-done | bytes 1638416 | tf_op jit(solution)/shard_map/all_gather | solution.py:380
  914.0 28.5 all-gather.55.cloned.1.call-done
  942.4 38.2 %all-gather.89.cloned.1.call-done = bf16[1,1376,1600]{1,2,0:T(8,128)(2,1)} async-done(((bf16[1,1376,200]{1,2,0:T(8,128)(2,1)}), bf16[1,1376,1600]{1,2,0:T(8,128)(2,1)}) %all-gather.89.cloned.1.call-update) | async-done | bytes 4403216 | tf_op jit(solution)/shard_map/all_gather | solution.py:187
  1017.2 26.1 reduce-scatter.91.cloned.1.call-done
  1047.5 34.4 %reduce-scatter.89.cloned.1.call-done = bf16[128,1600]{1,0:T(8,128)(2,1)} async-done(((bf16[512,1600]{1,0:T(8,128)(2,1)}), bf16[128,1600]{1,0:T(8,128)(2,1)}) %reduce-scatter.89.cloned.1.call-update) | async-done | bytes 409616
  1155.9 52.4 %while.162 = (s32[]{:T(128)}, f32[800,16]{0,1:T(8,128)S(1)}, f32[8,800,16]{1,2,0:T(8,128)}, f32[8,64,800]{2,1,0:T(8,128)}, s32[8,64]{1,0:T(8,128)S(1)}, /*index=...) while((s32[]{:T(128)}, f32[800,16]{0,1:T(8,128)S(1)}, ...), condition=%wide.region_39.41_spmd.clone, body=%wide.region_38.40_spmd.clone.sunk | while | flops 10036197 | bytes 700162 | solution.py:160
  1211.2 180.8 %while.156 = (s32[]{:T(128)}, f32[800,16]{0,1:T(8,128)S(1)}, f32[8,64,800]{2,1,0:T(8,128)}, f32[8,64,800]{2,1,0:T(8,128)}, f32[8,64,16]{1,0,2:T(8,128)S(1)}, /*i...) while((s32[]{:T(128)}, f32[800,16]{0,1:T(8,128)S(1)}, ...), condition=%wide.region_47.49_spmd.clone, body=%wide.region_40.48_spmd.clone.sunk | while | flops 95554592 | bytes 7363457 | solution.py:160
  1497.0 37.4 %all-gather.59.cloned.1.call-done = bf16[512,1600]{0,1:T(8,128)(2,1)} async-done(((bf16[128,1600]{0,1:T(8,128)(2,1)}), bf16[512,1600]{0,1:T(8,128)(2,1)}) %all-gather.59.cloned.1.call-update) | async-done | bytes 1638416 | tf_op jit(solution)/shard_map/all_gather | solution.py:210
  1556.2 35.5 %reduce-scatter.97.cloned.1.call-done = bf16[128,1600]{1,0:T(8,128)(2,1)} async-done(((bf16[512,1600]{1,0:T(8,128)(2,1)}), bf16[128,1600]{1,0:T(8,128)(2,1)}) %reduce-scatter.97.cloned.1.call-update) | async-done | bytes 409616
  1715.8 29.1 copy.591
  1794.6 53.1 %while.163 = (s32[]{:T(128)}, f32[800,16]{0,1:T(8,128)S(1)}, f32[8,800,16]{1,2,0:T(8,128)S(1)}, f32[8,64,800]{2,1,0:T(8,128)}, s32[8,64]{1,0:T(8,128)}, /*index=...) while((s32[]{:T(128)}, f32[800,16]{0,1:T(8,128)S(1)}, ...), condition=%wide.region_63.65_spmd.clone, body=%wide.region_62.64_spmd.clone.sunk | while | flops 10036197 | bytes 706306 | solution.py:160
  1850.5 181.0 %while.157 = (s32[]{:T(128)}, f32[800,16]{0,1:T(8,128)S(1)}, f32[8,64,800]{2,1,0:T(8,128)}, f32[8,64,800]{2,1,0:T(8,128)}, f32[8,64,16]{1,0,2:T(8,128)S(1)}, /*i...) while((s32[]{:T(128)}, f32[800,16]{0,1:T(8,128)S(1)}, ...), condition=%wide.region_71.73_spmd.clone, body=%wide.region_64.72_spmd.clone.sunk | while | flops 95554592 | bytes 7363457 | solution.py:160
  2094.9 29.1 copy.592
  2179.4 34.4 %reduce-scatter.105.cloned.1.call-done = bf16[400,3]{1,0:T(8,128)(2,1)} async-done(((bf16[3200,3]{1,0:T(8,128)(2,1)}), bf16[400,3]{1,0:T(8,128)(2,1)}) %reduce-scatter.105.cloned.1.call-update) | async-done | bytes 2416
  2215.0 37.1 %reduce-scatter.103.cloned.1.call-done = bf16[400,3]{1,0:T(8,128)(2,1)} async-done(((bf16[3200,3]{1,0:T(8,128)(2,1)}), bf16[400,3]{1,0:T(8,128)(2,1)}) %reduce-scatter.103.cloned.1.call-update) | async-done | bytes 2416
  2253.2 62.4 %reduce-scatter.125.cloned.1.call-done = bf16[1,1376,200]{1,2,0:T(8,128)(2,1)} async-done(((bf16[1,1376,1600]{1,2,0:T(8,128)(2,1)}), bf16[1,1376,200]{1,2,0:T(8,128)(2,1)}) %reduce-scatter.125.cloned.1.call-update) | async-done | bytes 550416
  2315.6 63.3 %reduce-scatter.123.cloned.1.call-done = bf16[1,1376,200]{1,2,0:T(8,128)(2,1)} async-done(((bf16[1,1376,1600]{1,2,0:T(8,128)(2,1)}), bf16[1,1376,200]{1,2,0:T(8,128)(2,1)}) %reduce-scatter.123.cloned.1.call-update) | async-done | bytes 550416
  2381.6 37.4 %reduce-scatter.99.cloned.1.call-done = bf16[128,1600]{1,0:T(8,128)(2,1)} async-done(((bf16[512,1600]{1,0:T(8,128)(2,1)}), bf16[128,1600]{1,0:T(8,128)(2,1)}) %reduce-scatter.99.cloned.1.call-update) | async-done | bytes 409616
  2451.2 48.8 %reduce-scatter.107.cloned.1.call-done = bf16[200,2752]{1,0:T(8,128)(2,1)} async-done(((bf16[1600,2752]{1,0:T(8,128)(2,1)}), bf16[200,2752]{1,0:T(8,128)(2,1)}) %reduce-scatter.107.cloned.1.call-update) | async-done | bytes 1100816
  2508.0 118.6 %all-reduce.37.cloned.1.call-done = (bf16[1,200,1600]{2,1,0:T(8,128)(2,1)}, bf16[1,200,1600]{2,1,0:T(8,128)(2,1)}, bf16[1,200,640]{2,1,0:T(8,128)(2,1)}, bf16[1,...) async-done(((bf16[1,200,1600]{2,1,0:T(8,128)(2,1)}, bf16[1,200,1600]{2,1,0:T(8,128)(2,1)}, bf16[1,200,640]{2,1,0:T(8,128)(2,1)}, ...) | async-done | bytes 3072016 | tf_op jit(solution)/shard_map/psum | solution.py:247
  2632.2 270.8 %all-reduce.35.cloned.1.call-done = (bf16[1,1600,3,800]{1,3,2,0:T(8,128)(2,1)}, bf16[1,1600,3,800]{1,3,2,0:T(8,128)(2,1)}, bf16[1,1600,32]{1,2,0:T(8,128)(2,1)},...) async-done(((bf16[1,1600,3,800]{1,3,2,0:T(8,128)(2,1)}, bf16[1,1600,3,800]{1,3,2,0:T(8,128)(2,1)}, ...) | async-done | bytes 20684816
  (1719 shorter events, 1622.4 us)
Async XLA Ops:
  15.5 238.5 %all-gather.71.cloned.1.call-start = ((), (), s32[]{:S(2)}) async-start(), calls=%async_computation.34 | async-start | bytes 3225600 | tf_op jit(solution)/shard_map/all_gather | solution.py:185
  16.5 251.0 %all-gather.63.cloned.1.call-start = ((), (), s32[]{:S(2)}) async-start(), calls=%async_computation.30 | async-start | bytes 2304000 | tf_op jit(solution)/shard_map/all_gather | solution.py:182
  17.4 302.6 %all-gather.65.cloned.1.call-start = ((), (), s32[]{:S(2)}) async-start(), calls=%async_computation.31 | async-start | bytes 5990400 | tf_op jit(solution)/shard_map/all_gather | solution.py:181
  18.7 335.0 %all-gather.67.cloned.1.call-start = ((), (), s32[]{:S(2)}) async-start(), calls=%async_computation.32 | async-start | bytes 5990400 | tf_op jit(solution)/shard_map/all_gather | solution.py:183
  20.4 338.3 %reduce-scatter.83.cloned.1.call-start = ((), (), s32[]{:S(2)}) async-start(), calls=%async_computation.44 | async-start | bytes 2129920
  267.2 144.0 %all-gather.49.cloned.1.call-start = ((), (), s32[]{:S(2)}) async-start(), calls=%async_computation.23 | async-start | bytes 2048000 | tf_op jit(solution)/shard_map/all_gather | solution.py:380
  363.9 131.2 %reduce-scatter.85.cloned.1.call-start = ((), (), s32[]{:S(2)}) async-start(), calls=%async_computation.45 | async-start | bytes 2129920
  458.2 133.4 %all-gather.51.cloned.1.call-start = ((), (), s32[]{:S(2)}) async-start(), calls=%async_computation.24 | async-start | bytes 2048000 | tf_op jit(solution)/shard_map/all_gather | solution.py:328
  497.7 251.8 %all-gather.85.cloned.1.call-start = ((), (), s32[]{:S(2)}) async-start(), calls=%async_computation.41 | async-start | bytes 3225600 | tf_op jit(solution)/shard_map/all_gather | solution.py:185
  498.3 261.9 %all-gather.77.cloned.1.call-start = ((), (), s32[]{:S(2)}) async-start(), calls=%async_computation.37 | async-start | bytes 2304000 | tf_op jit(solution)/shard_map/all_gather | solution.py:182
  498.8 293.9 %all-gather.79.cloned.1.call-start = ((), (), s32[]{:S(2)}) async-start(), calls=%async_computation.38 | async-start | bytes 5990400 | tf_op jit(solution)/shard_map/all_gather | solution.py:181
  499.4 345.3 %all-gather.81.cloned.1.call-start = ((), (), s32[]{:S(2)}) async-start(), calls=%async_computation.39 | async-start | bytes 5990400 | tf_op jit(solution)/shard_map/all_gather | solution.py:183
  500.0 349.6 %reduce-scatter.87.cloned.1.call-start = ((), (), s32[]{:S(2)}) async-start(), calls=%async_computation.46 | async-start | bytes 2129920
  760.1 143.7 %all-gather.53.cloned.1.call-start = ((), (), s32[]{:S(2)}) async-start(), calls=%async_computation.25 | async-start | bytes 2048000 | tf_op jit(solution)/shard_map/all_gather | solution.py:380
  856.7 186.5 %reduce-scatter.91.cloned.1.call-start = ((), (), s32[]{:S(2)}) async-start(), calls=%async_computation.48 | async-start | bytes 2129920
  1088.7 382.3 %reduce-scatter.93.cloned.1.call-start = ((), (), s32[]{:S(2)}) async-start(), calls=%async_computation.49 | async-start | bytes 2129920
  1556.0 132.6 %reduce-scatter.101.cloned.1.call-start = ((), (), s32[]{:S(2)}) async-start(), calls=%async_computation.53 | async-start | bytes 819200
  1661.3 481.9 %reduce-scatter.117.cloned.1.call-start = ((), (), s32[]{:S(2)}) async-start(), calls=%async_computation.61 | async-start | bytes 2304000
  1663.4 479.8 %reduce-scatter.113.cloned.1.call-start = ((), (), s32[]{:S(2)}) async-start(), calls=%async_computation.59 | async-start | bytes 5990400
  1667.6 475.6 %reduce-scatter.121.cloned.1.call-start = ((), (), s32[]{:S(2)}) async-start(), calls=%async_computation.63 | async-start | bytes 5990400
  1672.7 470.5 %reduce-scatter.115.cloned.1.call-start = ((), (), s32[]{:S(2)}) async-start(), calls=%async_computation.60 | async-start | bytes 2304000
  1691.5 451.7 %reduce-scatter.111.cloned.1.call-start = ((), (), s32[]{:S(2)}) async-start(), calls=%async_computation.58 | async-start | bytes 5990400
  1701.8 441.5 %reduce-scatter.119.cloned.1.call-start = ((), (), s32[]{:S(2)}) async-start(), calls=%async_computation.62 | async-start | bytes 5990400
  1706.6 469.4 %reduce-scatter.109.cloned.1.call-start = ((), (), s32[]{:S(2)}) async-start(), calls=%async_computation.57 | async-start | bytes 10137600
  1764.0 449.9 %reduce-scatter.105.cloned.1.call-start = ((), (), s32[]{:S(2)}) async-start(), calls=%async_computation.55 | async-start | bytes 921600
  2050.0 202.0 %reduce-scatter.103.cloned.1.call-start = ((), (), s32[]{:S(2)}) async-start(), calls=%async_computation.54 | async-start | bytes 921600
  2055.7 259.8 %reduce-scatter.125.cloned.1.call-start = ((), (), s32[]{:S(2)}) async-start(), calls=%async_computation.65 | async-start | bytes 5068800
  2063.0 315.8 %reduce-scatter.123.cloned.1.call-start = ((), (), s32[]{:S(2)}) async-start(), calls=%async_computation.64 | async-start | bytes 5068800
  2070.0 348.9 %reduce-scatter.99.cloned.1.call-start = ((), (), s32[]{:S(2)}) async-start(), calls=%async_computation.52 | async-start | bytes 2129920
  2086.4 413.5 %reduce-scatter.107.cloned.1.call-start = ((), (), s32[]{:S(2)}) async-start(), calls=%async_computation.56 | async-start | bytes 10137600
  2143.1 483.5 %all-reduce.37.cloned.1.call-start = ((), (), s32[]{:S(2)}) async-start(), calls=%async_computation.67 | async-start | bytes 6348800 | tf_op jit(solution)/shard_map/psum | solution.py:247
  2143.7 759.3 %all-reduce.35.cloned.1.call-start = ((), (), s32[]{:S(2)}) async-start(), calls=%async_computation.66 | async-start | bytes 43024384
  (221 other events, 7993.2 us)
Sparse Core Ops, SparseCore 0:
  12.4 43.1 all-gather.46
  58.1 51.8 all-gather.68
  175.4 41.4 all-gather.64
  218.6 41.7 all-gather.66
  263.7 47.8 reduce-scatter.82
  314.2 56.0 all-gather.72
  372.4 38.7 all-gather.48
  457.7 37.3 reduce-scatter.84
  496.8 54.3 all-gather.82
  552.8 38.7 all-gather.50
  654.6 41.7 all-gather.78
  698.0 41.8 all-gather.80
  759.0 46.0 reduce-scatter.86
  807.0 56.0 all-gather.86
  865.0 38.7 all-gather.52
  1005.9 37.3 reduce-scatter.90
  1088.9 37.8 all-gather.56
  1496.7 37.6 all-gather.58
  1690.2 37.6 all-gather.60
  1732.0 41.2 reduce-scatter.116
  1776.9 64.7 reduce-scatter.112
  1845.2 64.7 reduce-scatter.120
  1914.4 43.0 reduce-scatter.114
  1960.8 64.8 reduce-scatter.110
  2029.3 64.8 reduce-scatter.118
  2097.7 78.3 reduce-scatter.108
  2256.0 59.5 reduce-scatter.124
  2319.3 59.4 reduce-scatter.122
  2381.6 37.3 reduce-scatter.98
  2422.5 77.4 reduce-scatter.106
  2502.6 123.9 all-reduce.36
  2632.5 270.4 all-reduce.34
  (14 shorter events, 454.9 us)
where the time goes:
time: 2970 us; the launch traced here: 2950 us
  waiting for transfers between devices  1320 us (44%)
  matrix products  522 us (18%)
  other arithmetic  485 us (16%)
  local copies, waits for them, and re-layouts  424 us (14%)
  blocking collectives  151 us (5%)
    unnamed x69, waiting for transfers between devices  725 us
    unnamed x461, local copies, waits for them, and re-layouts  214 us
    reduce_sum x16, other arithmetic, block_step(): gap_b = run_b[:, None, :] - run_b[None, :, :]  166 us
    psum x1, waiting for transfers between devices, reduce_grads(): lax.psum(shards[0].astype(jnp.bfloat16), 'tp').astype(jnp.float32)  119 us
    all_gather x2, waiting for transfers between devices, fetch_weights(): lax.all_gather(input_weight[layer_index], 'fsdp', axis=0, tiled=True)  103 us
    all_gather x4, waiting for transfers between devices, spread_rows(): return lax.all_gather(values, 'tp', axis=0, tiled=True)  86.9 us
    all_gather x2, waiting for transfers between devices, forward_layer(): lax.all_gather(feedforward_input, 'tp', axis=0, tiled=True)  81.7 us
    reduce_sum x16, other arithmetic, block_step(): jnp.sum(decay_pairs * inner_bc[:, :, None] * in_b[None, :, :], axis=1)  77.7 us
  transfers between devices with their start and end apart: 54, of which 32 were waited for; matrix products, arithmetic and copies ran while one was open for 33% of the time, Pallas kernels for 0%

commit v1 on v0

v1 whole, which is shorter than its diff:
```python
import functools

import jax
import jax.numpy as jnp
from jax import lax
from jax.experimental import pallas as pl
from jax.experimental.pallas import tpu as pltpu
from jax.sharding import Mesh
from jax.sharding import PartitionSpec as P

HEADS = 25
HEAD = 64
KV_HEADS = 5
GROUP = HEADS // KV_HEADS
WINDOW = 1024
STATE = 16
EPSILON = 1e-05
TOP_PRECISION = lax.Precision.HIGHEST

CORES = 2
CHUNKS = 8
AT_ONCE = 4
LANES = 128
SLOTS = 2
VMEM_BYTES = 56 * 1024 * 1024
F32 = jnp.float32
BF16 = jnp.bfloat16


def round_up(value, unit):
    return -(-value // unit) * unit


def dot(a, b, out=F32):
    return jnp.dot(a, b, preferred_element_type=F32).astype(out)


def dot_nt(a, b, out=F32):
    return lax.dot_general(
        a, b, (((1,), (1,)), ((), ())), preferred_element_type=F32
    ).astype(out)


def dot_tn(a, b, out=F32):
    return lax.dot_general(
        a, b, (((0,), (0,)), ((), ())), preferred_element_type=F32
    ).astype(out)


def rms_scale(values, gain_row):
    return (
        values * lax.rsqrt(jnp.mean(values * values, axis=-1, keepdims=True) + EPSILON) * gain_row
    )


def branch_mix(attn_out, mamba_out, gain_attn, gain_mamba):
    return 0.5 * (rms_scale(attn_out, gain_attn) + rms_scale(mamba_out, gain_mamba))


def swiglu(gate_up_product):
    half = gate_up_product.shape[1] // 2
    return jax.nn.silu(gate_up_product[:, :half]) * gate_up_product[:, half:]


def softplus(v):
    return jnp.maximum(v, 0.0) + jnp.log1p(jnp.exp(-jnp.abs(v)))


def sigmoid(v):
    return 1.0 / (1.0 + jnp.exp(-v))


def kernel_params(bytes_limit=VMEM_BYTES):
    return pltpu.CompilerParams(
        dimension_semantics=("arbitrary",), vmem_limit_bytes=bytes_limit
    )


def cost(flops, moved):
    return pl.CostEstimate(flops=int(flops), bytes_accessed=int(moved), transcendentals=0)


def spread_bc(bc_ref, spread, turned, length):
    def turn(s, carry):
        place = pl.ds(pl.multiple_of(s * CHUNKS, CHUNKS), CHUNKS)
        turned[place, :] = bc_ref[pl.ds(s, CHUNKS, stride=length), :]
        return carry

    lax.fori_loop(0, length, turn, 0, unroll=8)
    block = 2 * LANES
    for q in range(2 * STATE * LANES // block):
        row = lax.broadcasted_iota(jnp.int32, (LANES, block), 0)
        column = lax.broadcasted_iota(jnp.int32, (LANES, block), 1) + q * block
        pick = (row == column // LANES).astype(F32).astype(BF16)
        for r in range(CHUNKS * length // block):
            part = slice(r * block, (r + 1) * block)
            spread[part, q * block : (q + 1) * block] = jnp.dot(
                turned[part, :].astype(BF16), pick, preferred_element_type=F32
            )


def spread_at(spread, s, n):
    place = pl.ds(pl.multiple_of(s * CHUNKS, CHUNKS), CHUNKS)
    return spread[place, n * LANES : (n + 1) * LANES]


def wide_lanes(t):
    return slice(t * LANES, (t + 1) * LANES)


def put(ref, value):
    for t in range(ref.shape[0]):
        ref[t] = value[:, wide_lanes(t)]


def get(ref, rows):
    return jnp.concatenate([ref[t, rows, :] for t in range(ref.shape[0])], axis=1)


def put_rows(ref, rows, value):
    for t in range(ref.shape[0]):
        ref[t, rows, :] = value[:, wide_lanes(t)]


def fill_decay(u_ref, pre_ref, keep_ref, par_ref, decay, inflow, count):
    step = softplus(pre_ref[...] + par_ref[1:2, :])
    keep = jnp.concatenate([keep_ref[...]] * count, axis=1)
    put(decay, jnp.exp(-step * jnp.exp(par_ref[0:1, :])) * keep)
    if u_ref is not None:
        put(inflow, step * u_ref[...])


def state_at(n):
    return slice(n * CHUNKS, (n + 1) * CHUNKS)


def stepped(refs, rows):
    return [[[ref[t, part, :] for t in range(ref.shape[0])] for part in rows] for ref in refs]


def before_kernel(length, count, me_ref, u_ref, pre_ref, bc_ref, keep_ref, par_ref, ends_ref, tail_ref, dev_ref, decay, inflow, ends):
    fill_decay(u_ref, pre_ref, keep_ref, par_ref, decay, inflow, count)

    def walk(k, rest):
        rows = pl.ds(length - 1 - k, CHUNKS, stride=length)
        for t in range(count):
            inflow[t, rows, :] = inflow[t, rows, :] * rest[t]
        return tuple(rest[t] * decay[t, rows, :] for t in range(count))

    ones = jnp.ones((CHUNKS, LANES), F32)
    rest = lax.fori_loop(0, length, walk, (ones,) * count, unroll=8)
    tail_ref[...] = jnp.concatenate(rest, axis=1)
    for r in range(CHUNKS):
        part = pl.ds(r * length, length)
        end = lax.dot_general(
            bc_ref[part, :].astype(BF16),
            get(inflow, part).astype(BF16),
            (((0,), (0,)), ((), ())),
            preferred_element_type=F32,
        )
        put_rows(ends, pl.ds(r, STATE, stride=CHUNKS), end[:STATE])
    ends_ref[...] = get(ends, slice(None))
    state = jnp.zeros((STATE, count * LANES), F32)
    total = jnp.ones((1, count * LANES), F32)
    for j in range(CHUNKS):
        r = me_ref[0] ^ j
        fade = tail_ref[pl.ds(r, 1), :]
        state = fade * state + get(ends, pl.ds(r, STATE, stride=CHUNKS))
        total = total * fade
    dev_ref[0:STATE, :] = state
    dev_ref[STATE : STATE + 8, :] = jnp.broadcast_to(total, (8, count * LANES))


def scan_kernel(
    length, count, me_ref, u_ref, gate_ref, pre_ref, bc_ref, keep_ref, par_ref, ends_ref, tail_ref, carried_ref,
    mid_ref, scanned_ref, start_ref, spread, turned, decay, inflow, scanned, ends, start,
):
    @pl.when(pl.program_id(0) == 0)
    def _():
        spread_bc(bc_ref, spread, turned, length)

    fill_decay(u_ref, pre_ref, keep_ref, par_ref, decay, inflow, count)
    put(ends, ends_ref[...])
    state = carried_ref[...]
    for j in range(CHUNKS):
        r = me_ref[0] ^ j
        rows = pl.ds(r, STATE, stride=CHUNKS)
        put_rows(start, rows, state)
        state = tail_ref[pl.ds(r, 1), :] * state + get(ends, rows)
    start_ref[...] = get(start, slice(None))

    def walk(i, carry):
        steps = [i * AT_ONCE + k for k in range(AT_ONCE)]
        rows = [pl.ds(s, CHUNKS, stride=length) for s in steps]
        a, x = stepped((decay, inflow), rows)
        sums = [[None] * count for _ in steps]
        for n in range(STATE):
            b = [spread_at(spread, s, n) for s in steps]
            c = [spread_at(spread, s, STATE + n) for s in steps]
            for t in range(count):
                h = start[t, state_at(n), :]
                for k in range(AT_ONCE):
                    h = a[k][t] * h + x[k][t] * b[k]
                    term = h * c[k]
                    sums[k][t] = term if n == 0 else sums[k][t] + term
                start[t, state_at(n), :] = h
        for k, part in enumerate(rows):
            for t in range(count):
                scanned[t, part, :] = sums[k][t]
        return carry

    lax.fori_loop(0, length // AT_ONCE, walk, 0)
    gate = gate_ref[...]
    y = get(scanned, slice(None))
    scanned_ref[...] = y
    mid_ref[...] = ((y + par_ref[2:3, :] * u_ref[...]) * (gate * sigmoid(gate))).astype(BF16)


def after_kernel(length, count, me_ref, grad_ref, gate_ref, pre_ref, bc_ref, keep_ref, par_ref, tail_ref, heads_ref, dev_ref, decay, flow, heads):
    fill_decay(None, pre_ref, keep_ref, par_ref, decay, None, count)
    gate = gate_ref[...]
    put(flow, grad_ref[...] * (gate * sigmoid(gate)))

    def walk(s, run):
        rows = pl.ds(s, CHUNKS, stride=length)
        new = []
        for t in range(count):
            new.append(run[t] * decay[t, rows, :])
            flow[t, rows, :] = flow[t, rows, :] * new[t]
        return tuple(new)

    lax.fori_loop(0, length, walk, (jnp.ones((CHUNKS, LANES), F32),) * count, unroll=8)
    for r in range(CHUNKS):
        part = pl.ds(r * length, length)
        head = lax.dot_general(
            bc_ref[part, :].astype(BF16),
            get(flow, part).astype(BF16),
            (((0,), (0,)), ((), ())),
            preferred_element_type=F32,
        )
        put_rows(heads, pl.ds(r, STATE, stride=CHUNKS), head[STATE : 2 * STATE])
    heads_ref[...] = get(heads, slice(None))
    state = jnp.zeros((STATE, count * LANES), F32)
    for j in range(CHUNKS - 1, -1, -1):
        r = me_ref[0] ^ j
        state = tail_ref[pl.ds(r, 1), :] * state + get(heads, pl.ds(r, STATE, stride=CHUNKS))
    dev_ref[...] = state


def scan_back_kernel(
    length, count, me_ref, grad_ref, u_ref, gate_ref, pre_ref, bc_ref, keep_ref, par_ref, tail_ref, scanned_ref, start_ref,
    heads_ref, carried_ref, pick_b_ref, pick_c_ref,
    gu_ref, gz_ref, gp_ref, gbc_ref, gpar_ref,
    spread, products, decay, inflow, flow, gx, glog, packed, later, heads, start, mixed, log_sum,
):
    @pl.when(pl.program_id(0) == 0)
    def _():
        spread_bc(bc_ref, spread, mixed, length)
        mixed[...] = jnp.zeros_like(mixed)

    fill_decay(u_ref, pre_ref, keep_ref, par_ref, decay, inflow, count)
    gate = gate_ref[...]
    g = grad_ref[...] * (gate * sigmoid(gate))
    put(flow, g)
    put(gx, g * scanned_ref[...])
    put(heads, heads_ref[...])
    put(start, start_ref[...])
    state = carried_ref[...]
    for j in range(CHUNKS - 1, -1, -1):
        r = me_ref[0] ^ j
        rows = pl.ds(r, STATE, stride=CHUNKS)
        put_rows(later, rows, state)
        state = tail_ref[pl.ds(r, 1), :] * state + get(heads, rows)

    def keep_products(i, n, terms):
        for k in range(0, AT_ONCE, 2):
            place = pl.ds(pl.multiple_of((i * AT_ONCE + k) * CHUNKS, 2 * CHUNKS), 2 * CHUNKS)
            products[place, n * LANES : (n + 1) * LANES] = jnp.concatenate(
                terms[k : k + 2], axis=0
            ).astype(BF16)

    def forward(i, carry):
        steps = [i * AT_ONCE + k for k in range(AT_ONCE)]
        rows = [pl.ds(s, CHUNKS, stride=length) for s in steps]
        a, x, g = stepped((decay, inflow, flow), rows)
        (yg,) = stepped((gx,), rows)
        for k, s in enumerate(steps):
            place = pl.ds(pl.multiple_of(s * CHUNKS, CHUNKS), CHUNKS)
            for index, value in enumerate((a, x, g, yg)):
                for t in range(count):
                    packed[index, t, place, :] = value[k][t]
        for n in range(STATE):
            b = [spread_at(spread, s, n) for s in steps]
            terms = [None] * AT_ONCE
            for t in range(count):
                h = start[t, state_at(n), :]
                for k in range(AT_ONCE):
                    h = a[k][t] * h + x[k][t] * b[k]
                    term = h * g[k][t]
                    terms[k] = term if t == 0 else terms[k] + term
                start[t, state_at(n), :] = h
            keep_products(i, n, terms)
        return carry

    lax.fori_loop(0, length // AT_ONCE, forward, 0)
    mixed[...] += jnp.dot(products[...], pick_c_ref[...], preferred_element_type=F32)
    for t in range(count):
        edge = later[t, state_at(0), :] * start[t, state_at(0), :]
        for n in range(1, STATE):
            edge = edge + later[t, state_at(n), :] * start[t, state_at(n), :]
        log_sum[t] = edge

    def backward(k, carry):
        i = length // AT_ONCE - 1 - k
        steps = [i * AT_ONCE + k for k in range(AT_ONCE)]
        places = [pl.ds(pl.multiple_of(s * CHUNKS, CHUNKS), CHUNKS) for s in steps]
        a, x, g = stepped((packed.at[0], packed.at[1], packed.at[2]), places)
        sums = [[None] * count for _ in steps]
        for n in range(STATE):
            b = [spread_at(spread, s, n) for s in steps]
            c = [spread_at(spread, s, STATE + n) for s in steps]
            terms = [None] * AT_ONCE
            for t in range(count):
                held = later[t, state_at(n), :]
                for k in range(AT_ONCE - 1, -1, -1):
                    adj = held + g[k][t] * c[k]
                    term = adj * b[k]
                    sums[k][t] = term if n == 0 else sums[k][t] + term
                    term = adj * x[k][t]
                    terms[k] = term if t == 0 else terms[k] + term
                    held = a[k][t] * adj
                later[t, state_at(n), :] = held
            keep_products(i, n, terms)
        for t in range(count):
            total = log_sum[t]
            for k in range(AT_ONCE - 1, -1, -1):
                target = pl.ds(steps[k], CHUNKS, stride=length)
                dx = sums[k][t]
                total = total + packed[3, t, places[k], :] - x[k][t] * dx
                total = jnp.where(a[k][t] == 0.0, 0.0, total)
                gx[t, target, :] = dx
                glog[t, target, :] = total
            log_sum[t] = total
        return carry

    lax.fori_loop(0, length // AT_ONCE, backward, 0)
    mixed[...] += jnp.dot(products[...], pick_b_ref[...], preferred_element_type=F32)

    @pl.when(pl.program_id(0) == pl.num_programs(0) - 1)
    def _():
        for j in range(CHUNKS):
            gbc_ref[j * length : (j + 1) * length, :] = mixed[
                pl.ds(j, length, stride=CHUNKS), :
            ].astype(BF16)

    rate = -jnp.exp(par_ref[0:1, :])
    skip = par_ref[2:3, :]
    u = u_ref[...]
    raw = pre_ref[...] + par_ref[1:2, :]
    step = softplus(raw)
    dx = get(gx, slice(None))
    dlog = get(glog, slice(None))
    gpre = (dlog * rate + dx * u) * sigmoid(raw)
    sig = sigmoid(gate)
    gu_ref[...] = (g * skip + dx * step).astype(BF16)
    gz_ref[...] = (
        grad_ref[...] * (scanned_ref[...] + skip * u) * (sig * (1.0 + gate * (1.0 - sig)))
    ).astype(BF16)
    gp_ref[...] = gpre.astype(BF16)
    gpar_ref[0:1, :] = jnp.sum(dlog * step, axis=0, keepdims=True) * rate
    gpar_ref[1:2, :] = jnp.sum(gpre, axis=0, keepdims=True)
    gpar_ref[2:3, :] = jnp.sum(g * u, axis=0, keepdims=True)
    gpar_ref[3:8, :] = jnp.zeros((5, count * LANES), F32)


class ScanCalls:
    def __init__(self, rows, wide, me):
        self.rows, self.wide, self.me = rows, wide, me
        self.length = rows // CHUNKS
        tiles = wide // LANES
        self.count = 2 if tiles % 2 == 0 else 1
        self.lanes = self.count * LANES
        self.steps = tiles // self.count
        self.bc_spec = pl.BlockSpec((rows, LANES), lambda t: (0, 3 * tiles))
        self.keep_spec = pl.BlockSpec((rows, LANES), lambda t: (0, 0))
        self.tile = pltpu.VMEM((self.count, rows, LANES), F32)
        self.thin = pltpu.VMEM((rows, LANES), F32)
        self.spread = pltpu.VMEM((rows, 2 * STATE * LANES), F32)
        self.packed = STATE * CHUNKS
        self.states = pltpu.VMEM((self.count, self.packed, LANES), F32)

    def tall(self, part):
        steps = self.steps
        return pl.BlockSpec((self.rows, self.lanes), lambda t: (0, part * steps + t))

    def flat(self, height):
        return pl.BlockSpec((height, self.lanes), lambda t: (0, t))

    def out(self, height, kind=F32):
        return jax.ShapeDtypeStruct((height, self.wide), kind)

    def call(self, kernel, in_specs, out_specs, out_shape, scratch, flops, moved):
        return pl.pallas_call(
            functools.partial(kernel, self.length, self.count),
            grid=(self.steps,),
            in_specs=[pl.BlockSpec(memory_space=pltpu.SMEM)] + in_specs,
            out_specs=out_specs,
            out_shape=out_shape,
            scratch_shapes=scratch,
            compiler_params=kernel_params(),
            cost_estimate=cost(flops, moved),
        )

    def before(self, proj, keep, par):
        return self.call(
            before_kernel,
            [self.tall(0), self.tall(2), self.bc_spec, self.keep_spec, self.flat(8)],
            [self.flat(self.packed), self.flat(CHUNKS), self.flat(STATE + 8)],
            [self.out(self.packed), self.out(CHUNKS), self.out(STATE + 8)],
            [self.tile, self.tile, self.states],
            2e9,
            self.rows * self.wide * 8,
        )(self.me, proj, proj, proj, keep, par)

    def scan(self, proj, keep, par, ends, tail, carried):
        return self.call(
            scan_kernel,
            [self.tall(0), self.tall(1), self.tall(2), self.bc_spec, self.keep_spec, self.flat(8)]
            + [self.flat(self.packed), self.flat(CHUNKS), self.flat(STATE)],
            [self.tall(0), self.tall(0), self.flat(self.packed)],
            [self.out(self.rows, BF16), self.out(self.rows), self.out(self.packed)],
            [self.spread, self.thin, self.tile, self.tile, self.tile, self.states, self.states],
            8e9,
            self.rows * self.wide * 18,
        )(self.me, proj, proj, proj, proj, keep, par, ends, tail, carried)

    def after(self, grad_mid, proj, keep, par, tail):
        return self.call(
            after_kernel,
            [self.tall(0), self.tall(1), self.tall(2), self.bc_spec, self.keep_spec, self.flat(8)]
            + [self.flat(CHUNKS)],
            [self.flat(self.packed), self.flat(STATE)],
            [self.out(self.packed), self.out(STATE)],
            [self.tile, self.tile, self.states],
            2e9,
            self.rows * self.wide * 12,
        )(self.me, grad_mid, proj, proj, proj, keep, par, tail)

    def back(self, grad_mid, proj, keep, par, tail, scanned, start, heads, carried):
        lane = jnp.arange(STATE * LANES, dtype=jnp.int32)[:, None] // LANES
        column = jnp.arange(LANES, dtype=jnp.int32)[None, :]
        pick_b = (lane == column).astype(BF16)
        pick_c = (lane + STATE == column).astype(BF16)
        pick_spec = pl.BlockSpec((STATE * LANES, LANES), lambda t: (0, 0))
        products = pltpu.VMEM((self.rows, STATE * LANES), BF16)
        return self.call(
            scan_back_kernel,
            [self.tall(0), self.tall(0), self.tall(1), self.tall(2), self.bc_spec]
            + [self.keep_spec, self.flat(8), self.flat(CHUNKS), self.tall(0)]
            + [self.flat(self.packed), self.flat(self.packed), self.flat(STATE)]
            + [pick_spec, pick_spec],
            [self.tall(0), self.tall(0), self.tall(0), self.keep_spec, self.flat(8)],
            [self.out(self.rows, BF16)] * 3
            + [jax.ShapeDtypeStruct((self.rows, LANES), BF16), self.out(8)],
            [self.spread, products] + [self.tile] * 5
            + [pltpu.VMEM((4, self.count, self.rows, LANES), F32)]
            + [self.states] * 3 + [self.thin, pltpu.VMEM((self.count, CHUNKS, LANES), F32)],
            2e10,
            self.rows * self.wide * 30,
        )(self.me, grad_mid, proj, proj, proj, proj, keep, par, tail, scanned, start, heads, carried, pick_b, pick_c)


def scores_of(base, q, keys, low_ref):
    scores = lax.dot_general(q, keys, (((1,), (1,)), ((), ())), preferred_element_type=F32)
    place = lax.broadcasted_iota(jnp.int32, scores.shape, 1) + base
    own = lax.broadcasted_iota(jnp.int32, scores.shape, 0) + (base + WINDOW)
    return jnp.where((place >= low_ref[...]) & (place <= own), scores, -1e30)


def lay_out(me_ref, block, parts, kv):
    for k, part in enumerate(parts):
        for j in range(CHUNKS):
            source = pl.multiple_of((me_ref[0] ^ j) * block, block)
            kv[(k * CHUNKS + j) * block : (k * CHUNKS + j + 1) * block, :] = part[pl.ds(source, block), :]


def attend_kernel(heads, hops, me_ref, q_ref, *refs):
    parts, (low_ref, out_ref, log_ref, kv) = refs[: hops + 1], refs[hops + 1 :]
    block = q_ref.shape[0]

    @pl.when(pl.program_id(0) == 0)
    def _():
        lay_out(me_ref, block, parts, kv)

    base = (pl.program_id(0) ^ me_ref[0]) * block + (hops * CHUNKS * block - WINDOW)
    window = pl.ds(pl.multiple_of(base, LANES), WINDOW + block)
    keys = kv[window, :LANES]
    values = kv[window, LANES:]
    lane = lax.broadcasted_iota(jnp.int32, (block, LANES), 1)
    logs = jnp.zeros((block, LANES), F32)
    for h in range(heads):
        part = slice(h * LANES, (h + 1) * LANES)
        scores = scores_of(base, q_ref[:, part], keys, low_ref)
        top = jnp.max(scores, axis=1, keepdims=True)
        soft = jnp.exp(scores - top)
        total = jnp.sum(soft, axis=1, keepdims=True)
        mix = jnp.dot(soft.astype(BF16), values, preferred_element_type=F32)
        out_ref[:, part] = (mix * (1.0 / total)).astype(BF16)
        logs = jnp.where(lane == h, top + jnp.log(total), logs)
    log_ref[...] = logs


def attend_back_kernel(heads, hops, me_ref, q_ref, *refs):
    parts, refs = refs[: hops + 1], refs[hops + 1 :]
    low_ref, log_ref, grad_ref, gq_ref = refs[:4]
    gparts, (kv, gkv) = refs[4 : hops + 5], refs[hops + 5 :]
    block = q_ref.shape[0]

    @pl.when(pl.program_id(0) == 0)
    def _():
        lay_out(me_ref, block, parts, kv)
        gkv[...] = jnp.zeros_like(gkv)

    base = (pl.program_id(0) ^ me_ref[0]) * block + (hops * CHUNKS * block - WINDOW)
    window = pl.ds(pl.multiple_of(base, LANES), WINDOW + block)
    keys = kv[window, :LANES]
    values = kv[window, LANES:]
    turned = (((0,), (0,)), ((), ()))
    for h in range(heads):
        part = slice(h * LANES, (h + 1) * LANES)
        q = q_ref[:, part]
        grad = grad_ref[:, part]
        soft = jnp.exp(scores_of(base, q, keys, low_ref) - log_ref[:, h : h + 1])
        gsoft = lax.dot_general(grad, values, (((1,), (1,)), ((), ())), preferred_element_type=F32)
        delta = jnp.sum(soft * gsoft, axis=1, keepdims=True)
        gscore = (soft * (gsoft - delta)).astype(BF16)
        gq_ref[:, part] = (
            jnp.dot(gscore, keys, preferred_element_type=F32) * 0.125
        ).astype(BF16)
        gkv[window, :LANES] += lax.dot_general(gscore, q, turned, preferred_element_type=F32)
        gkv[window, LANES:] += lax.dot_general(
            soft.astype(BF16), grad, turned, preferred_element_type=F32
        )

    @pl.when(pl.program_id(0) == pl.num_programs(0) - 1)
    def _():
        for k, part in enumerate(gparts):
            for j in range(CHUNKS):
                target = pl.multiple_of((me_ref[0] ^ j) * block, block)
                part[pl.ds(target, block), :] = gkv[
                    (k * CHUNKS + j) * block : (k * CHUNKS + j + 1) * block, :
                ].astype(part.dtype)


def attend_specs(rows, hops):
    block = rows // CHUNKS
    by_row = lambda width: pl.BlockSpec((block, width), lambda b: (b, 0))
    whole = [pl.BlockSpec((rows, 2 * LANES), lambda b: (0, 0))] * (hops + 1)
    total = (hops + 1) * rows
    return by_row, whole, total, pl.BlockSpec(memory_space=pltpu.SMEM)


def attend(me, q, kvs, low):
    rows, wide = q.shape
    heads = wide // LANES
    by_row, whole, total, scalar = attend_specs(rows, len(kvs) - 1)
    return pl.pallas_call(
        functools.partial(attend_kernel, heads, len(kvs) - 1),
        grid=(CHUNKS,),
        in_specs=[scalar, by_row(wide), *whole, by_row(1)],
        out_specs=[by_row(wide), by_row(LANES)],
        out_shape=[
            jax.ShapeDtypeStruct((rows, wide), BF16),
            jax.ShapeDtypeStruct((rows, LANES), F32),
        ],
        scratch_shapes=[pltpu.VMEM((total, 2 * LANES), BF16)],
        compiler_params=kernel_params(),
        cost_estimate=cost(6e9, 8e6),
    )(me, q, *kvs, low)


def attend_back(me, q, kvs, low, logs, grad):
    rows, wide = q.shape
    heads = wide // LANES
    by_row, whole, total, scalar = attend_specs(rows, len(kvs) - 1)
    part = jax.ShapeDtypeStruct((rows, 2 * LANES), BF16)
    own = jax.ShapeDtypeStruct((rows, 2 * LANES), F32)
    return pl.pallas_call(
        functools.partial(attend_back_kernel, heads, len(kvs) - 1),
        grid=(CHUNKS,),
        in_specs=[scalar, by_row(wide), *whole, by_row(1), by_row(LANES), by_row(wide)],
        out_specs=[by_row(wide), *whole],
        out_shape=[jax.ShapeDtypeStruct((rows, wide), BF16)] + [part] * (len(kvs) - 1) + [own],
        scratch_shapes=[
            pltpu.VMEM((total, 2 * LANES), BF16),
            pltpu.VMEM((total, 2 * LANES), F32),
        ],
        compiler_params=kernel_params(),
        cost_estimate=cost(1.5e10, 1.2e7),
    )(me, q, *kvs, low, logs, grad)


def swap_cores(value):
    return lax.ppermute(value, "core", [(0, 1), (1, 0)])


def from_peer(value, k):
    return lax.ppermute(value, "tp", [(n, n ^ k) for n in range(lax.axis_size("tp"))])


def team_gather(rows):
    tps = lax.axis_size("tp")
    got = {k: from_peer(rows, k) for k in range(tps - 1, 0, -1)}
    own = jnp.concatenate([rows] + [got[k] for k in range(1, tps)], axis=0)
    return jnp.concatenate([own, swap_cores(own)], axis=0)


def team_scatter(values):
    tps = lax.axis_size("tp")
    half = values.shape[0] // CORES
    block = half // tps
    both = values[:half].astype(F32) + swap_cores(values[half:]).astype(F32)
    low = both.astype(BF16)
    got = [from_peer(low[k * block : (k + 1) * block], k) for k in range(tps - 1, 0, -1)]
    total = both[:block]
    for part in got:
        total = total + part.astype(F32)
    return total


def shifted(value, steps):
    count = lax.axis_size("chip")
    leading, last = (max(0, -steps), min(count, count - steps))
    return lax.ppermute(value, "chip", [(k, k + steps) for k in range(leading, last)])


def behind(value, other):
    first = other[(slice(0, 1),) * other.ndim].reshape((1,) * value.ndim)
    return value + (first * 0).astype(value.dtype)


def by_core(mine, other):
    first = lax.axis_index("core") == 0
    return jnp.where(first, mine, other), jnp.where(first, other, mine)


def to_rows(values):
    tps = lax.axis_size("tp")
    half = values.shape[0] // CORES
    block = half // tps
    pair = jnp.concatenate([values[:half], swap_cores(values[half:])], axis=1)
    got = [from_peer(pair[k * block : (k + 1) * block], k) for k in range(1, tps)]
    return jnp.concatenate([pair[:block]] + got, axis=1)


def to_columns(values):
    tps = lax.axis_size("tp")
    step = values.shape[1] // tps
    got = [from_peer(values[:, k * step : (k + 1) * step], k) for k in range(1, tps)]
    pair = jnp.concatenate([values[:, :step]] + got, axis=0)
    return jnp.concatenate([pair[:, : step // CORES], swap_cores(pair[:, step // CORES :])], axis=0)


def own_halves(shard, other=None):
    core = lax.axis_index("core")
    if other is not None:
        shard = behind(shard, other)
    mine = lax.dynamic_index_in_dim(shard, core, 1, False)
    other = swap_cores(lax.dynamic_index_in_dim(shard, 1 - core, 1, False))
    pair = jnp.concatenate(by_core(mine, other), axis=0)
    return lax.all_gather(pair, "chip", axis=0, tiled=True)


def summed_halves(full):
    rows = lax.psum_scatter(full, "chip", scatter_dimension=0, tiled=True)
    rows = rows.reshape(CORES, rows.shape[0] // CORES, -1)
    core = lax.axis_index("core")
    mine = lax.dynamic_index_in_dim(rows, core, 0, False)
    return mine, swap_cores(lax.dynamic_index_in_dim(rows, 1 - core, 0, False))


def share_columns(mine, other):
    tps = lax.axis_size("tp")
    pair = jnp.stack([mine, other])
    whole = jnp.concatenate([pair] + [from_peer(pair, k) for k in range(1, tps)], axis=0)
    own = lax.axis_index("tp") * CORES + lax.axis_index("core")
    return jnp.concatenate(
        [lax.dynamic_slice_in_dim(whole, own ^ k, 1, 0) for k in range(CORES * tps)], axis=0
    )


def body(
    x_in, lengths, w_q, w_kv, w_o, input_weight, a_log, dt_bias, d_skip,
    w_bc, w_out, gains, gate_up_weight, w_down, cotangent,
):
    chips, tps = lax.axis_size("chip"), lax.axis_size("tp")
    chip, core, tp = (lax.axis_index(name) for name in ("chip", "core", "tp"))
    team = CORES * tps
    unit = tp * CORES + core
    layers, shard_rows, width = w_q.shape
    rows_own = x_in.shape[0]
    rows = rows_own * team
    hops = -(-WINDOW // rows)
    kv_half = w_kv.shape[2] // 2
    heads_here = -(-HEADS // team)
    q_wide = heads_here * HEAD
    slot_wide = SLOTS * HEAD
    channels = a_log.shape[1] // CORES
    wide = round_up(channels, LANES)
    hidden_here = gate_up_weight.shape[3] // CORES
    out_wide = round_up(channels + width // CORES, LANES)
    ffn_wide = round_up(3 * hidden_here, LANES)
    me = (core * tps + tp).astype(jnp.int32)
    me_array = jnp.reshape(me, (1,))
    scan = ScanCalls(rows, wide, me_array)

    order = jnp.arange(team, dtype=jnp.int32) ^ me
    local = order[:, None] * rows_own + jnp.arange(rows_own, dtype=jnp.int32)[None, :]
    places = chip * rows + local.reshape(rows)
    starts = (jnp.cumsum(lengths) - lengths).astype(jnp.int32)
    reached = places[:, None] >= starts[None, :]
    opening = jnp.any(places[:, None] == starts[None, :], axis=1)
    keep = jnp.broadcast_to((1.0 - opening.astype(F32))[:, None], (rows, LANES))
    first = jnp.max(jnp.where(reached, starts[None, :], 0), axis=1)
    low = jnp.maximum(first, places - (WINDOW - 1)) - (chip - hops) * rows
    low = low[:, None]

    head_ids = unit * heads_here + jnp.arange(heads_here, dtype=jnp.int32)
    slot_ids = head_ids // GROUP - (unit * heads_here) // GROUP
    upper = (slot_ids == 1)[None, :, None]

    def pad_lanes(values, size):
        return jnp.pad(values, [(0, 0)] * (values.ndim - 1) + [(0, size - values.shape[-1])])

    def kv_columns(layer, index):
        base = (index * heads_here) // GROUP * HEAD
        whole = jnp.pad(w_kv[layer].reshape(shard_rows, 2, kv_half), ((0, 0), (0, 0), (0, slot_wide)))
        return lax.dynamic_slice_in_dim(whole, base, slot_wide, 2).reshape(shard_rows, 2 * slot_wide)

    def fetch_mixer_in(layer, lead=None):
        ins = input_weight[layer].reshape(shard_rows, 3, CORES, channels)
        ins = pad_lanes(ins.transpose(0, 2, 1, 3), wide).reshape(shard_rows, CORES, 3 * wide)
        qs = lax.dynamic_slice_in_dim(
            pad_lanes(w_q[layer], team * q_wide), tp * CORES * q_wide, CORES * q_wide, 1
        ).reshape(shard_rows, CORES, q_wide)
        kvs = jnp.stack([kv_columns(layer, tp * CORES + k) for k in range(CORES)], axis=1)
        full = own_halves(jnp.concatenate([ins, qs, kvs], axis=2), lead)
        return full[:, 3 * wide :], full[:, : 3 * wide]

    def fetch_mixer_out(layer, lead):
        outs = pad_lanes(w_out[layer].T.reshape(shard_rows, CORES, channels), wide)
        os = w_o[layer].reshape(shard_rows, CORES, width // CORES)
        os = pad_lanes(os, round_up(width // CORES, LANES))
        full = own_halves(jnp.concatenate([outs, os], axis=2), lead)
        o = jnp.pad(full[:, wide : wide + width // CORES], ((0, team * q_wide - width), (0, 0)))
        o = jnp.concatenate(
            [lax.dynamic_slice_in_dim(o, (unit ^ k) * q_wide, q_wide, 0) for k in range(team)], axis=0
        )
        blocks = swap_cores(o).reshape(tps, CORES, q_wide, -1)
        blocks = blocks[:, ::-1].reshape(o.shape)
        return full[:, :wide], jnp.concatenate(by_core(o, blocks), axis=1)

    def fetch_ffn(layer, lead):
        gus = gate_up_weight[layer].reshape(shard_rows, 2, CORES, hidden_here)
        gus = gus.transpose(0, 2, 1, 3).reshape(shard_rows, CORES, 2 * hidden_here)
        downs = w_down[layer].T.reshape(shard_rows, CORES, hidden_here)
        full = own_halves(pad_lanes(jnp.concatenate([gus, downs], axis=2), ffn_wide), lead)
        return full[:, : 2 * hidden_here], full[:, 2 * hidden_here : 3 * hidden_here]

    def scan_params(layer):
        mine = [
            lax.dynamic_slice_in_dim(part[layer], core * channels, channels, 0)
            for part in (a_log, dt_bias, d_skip)
        ]
        return jnp.pad(jnp.stack(mine), ((0, 5), (0, wide - channels)))

    def chain(everything, back):
        state = jnp.zeros(everything[0][0].shape, F32)
        order = range(chips - 1, -1, -1) if back else range(chips)
        for k in order:
            counts = (k > chip) if back else (k < chip)
            new = everything[1][k][None, :] * state + everything[0][k]
            state = jnp.where(counts, new, state)
        return state

    def slots(values):
        values = values.reshape(rows, heads_here, HEAD)
        nothing = jnp.zeros_like(values)
        return jnp.concatenate(
            [jnp.where(upper, nothing, values), jnp.where(upper, values, nothing)], axis=2
        ).reshape(rows, heads_here * slot_wide)

    def unslot(values):
        values = values.reshape(rows, heads_here, SLOTS, HEAD)
        return jnp.where(upper, values[:, :, 1], values[:, :, 0]).reshape(rows, q_wide)

    def forward_layer(stream, layer, weights):
        (w_attn, w_ssm), (w_mamba, w_attn_out), (w_gu, w_dn) = weights
        gain = gains[layer]
        par = scan_params(layer)
        normed = rms_scale(stream, gain[0]).astype(BF16)
        normed_all = team_gather(normed)
        qkv = dot(normed_all, w_attn, BF16)
        kv = qkv[:, q_wide:]
        kvs = [shifted(kv, hop) for hop in range(hops, 0, -1)] + [kv]
        bc = dot(normed_all, pad_lanes(w_bc[layer], LANES), BF16).astype(F32)
        proj = jnp.concatenate([dot(normed_all, w_ssm), bc], axis=1)
        ends, tail, dev = scan.before(proj, keep, par)
        devs = lax.all_gather(dev, "chip")
        chip_decay = devs[:, STATE]
        carried = chain((devs[:, :STATE], chip_decay), False)
        q = slots(qkv[:, :q_wide] * BF16(0.125))
        mix, logs = attend(me_array, q, kvs, low)
        attended = unslot(mix)
        attn_out = dot(to_rows(attended), w_attn_out)
        mid, scanned, start = scan.scan(proj, keep, behind(par, attended), ends, tail, carried)
        mamba_out = team_scatter(dot_nt(mid, w_mamba, BF16))
        middle = stream + branch_mix(attn_out, mamba_out, gain[1], gain[2])
        ffn_all = team_gather(rms_scale(middle, gain[3]).astype(BF16))
        gate_up = dot(ffn_all, w_gu)
        hidden = swiglu(gate_up).astype(BF16)
        ffn_out = team_scatter(dot_nt(hidden, w_dn, BF16))
        kept = dict(
            stream=stream, normed_all=normed_all, q=q, kvs=kvs, logs=logs,
            attended=attended, proj=proj, tail=tail, chip_decay=chip_decay, mid=mid,
            scanned=scanned, start=start, attn_out=attn_out, mamba_out=mamba_out, middle=middle,
            ffn_all=ffn_all, gate_up=gate_up, hidden=hidden, par=par,
        )
        return middle + ffn_out, kept

    def backward_layer(grad_out, layer, weights, kept):
        (w_attn, w_ssm), (w_mamba, w_attn_out), (w_gu, w_dn) = weights
        gain = gains[layer]
        normed_all = kept["normed_all"]
        grad_all = team_gather(grad_out.astype(BF16))
        grad_hidden = dot(grad_all, w_dn)
        _, swiglu_pull = jax.vjp(swiglu, kept["gate_up"])
        grad_gu = swiglu_pull(grad_hidden)[0].astype(BF16)
        grad_ffn = team_scatter(dot_nt(grad_gu, w_gu, BF16))
        ffn_sums = summed_halves(
            pad_lanes(
                jnp.concatenate(
                    [dot_tn(kept["ffn_all"], grad_gu, BF16), dot_tn(grad_all, kept["hidden"], BF16)],
                    axis=1,
                ),
                ffn_wide,
            )
        )
        _, norm_pull = jax.vjp(rms_scale, kept["middle"], gain[3])
        grad_mid_norm, grad_gain_ffn = norm_pull(grad_ffn)
        grad_middle = grad_out + grad_mid_norm
        _, mix_pull = jax.vjp(branch_mix, kept["attn_out"], kept["mamba_out"], gain[1], gain[2])
        grad_attn, grad_mamba, grad_gain_attn, grad_gain_mamba = mix_pull(grad_middle)
        grad_mamba_all = team_gather(grad_mamba.astype(BF16))
        grad_attn = grad_attn.astype(BF16)
        grad_att = slots(to_columns(dot_nt(grad_attn, w_attn_out, BF16)))
        grad_attn_all = team_gather(behind(grad_attn, grad_mamba_all))
        grad_mid = dot(grad_mamba_all, w_mamba)
        par = kept["par"]
        heads, dev = scan.after(grad_mid, kept["proj"], keep, par, kept["tail"])
        devs = lax.all_gather(dev, "chip")
        carried = chain((devs, kept["chip_decay"]), True)

        gq, *gkvs = attend_back(me_array, kept["q"], kept["kvs"], low, kept["logs"], grad_att)
        gkv = gkvs[hops]
        for hop in range(1, hops + 1):
            gkv = gkv + shifted(gkvs[hops - hop], -hop).astype(F32)
        grad_qkv = jnp.concatenate([unslot(gq), gkv.astype(BF16)], axis=1)
        attn_sums = summed_halves(
            jnp.concatenate(
                [
                    dot_tn(grad_mamba_all, kept["mid"], BF16),
                    dot_tn(grad_attn_all, kept["attended"], BF16),
                    dot_tn(normed_all, grad_qkv, BF16),
                ],
                axis=1,
            )
        )
        gu, gz, gp, gbc, gpar = scan.back(
            grad_mid, kept["proj"], keep, par, kept["tail"], kept["scanned"], kept["start"], heads, carried
        )
        grad_proj = jnp.concatenate([gu, gz, gp, gbc], axis=1)
        grad_normed = team_scatter(
            (
                dot_nt(grad_qkv, w_attn)
                + dot_nt(grad_proj[:, : 3 * wide], w_ssm)
                + dot_nt(gbc, pad_lanes(w_bc[layer], LANES))
            ).astype(BF16)
        )
        ssm_sums = summed_halves(dot_tn(normed_all, grad_proj, BF16))
        _, in_pull = jax.vjp(rms_scale, kept["stream"], gain[0])
        grad_stream_norm, grad_gain_in = in_pull(grad_normed)
        grad_gains = jnp.stack([grad_gain_in, grad_gain_attn, grad_gain_mamba, grad_gain_ffn])
        shared = share_columns(*(part[:, wide:] for part in attn_sums))
        shared_bc = share_columns(*(part[:, 3 * wide :] for part in ssm_sums))
        small = jnp.concatenate([grad_gains.reshape(-1), gpar[:3, :channels].reshape(-1)])
        return grad_middle + grad_stream_norm, (ffn_sums, attn_sums, ssm_sums, shared, shared_bc, small)

    weights = []
    lead = None
    for layer in range(layers):
        ins = fetch_mixer_in(layer, lead)
        lead = ins[0] if layer == 0 else lead
        weights.append((ins, fetch_mixer_out(layer, lead), fetch_ffn(layer, lead)))
    stream = x_in.astype(F32)
    kept = []
    for layer in range(layers):
        stream, saved = forward_layer(stream, layer, weights[layer])
        kept.append(saved)
    block_out = stream.astype(BF16)
    grad_stream = cotangent.astype(F32)
    sums = [None] * layers
    for layer in range(layers - 1, -1, -1):
        grad_stream, sums[layer] = backward_layer(grad_stream, layer, weights[layer], kept[layer])

    shared = jnp.stack([parts[3] for parts in sums]).transpose(0, 2, 1, 3)
    turned = shared[..., :q_wide].reshape(layers, shard_rows, team * q_wide)[..., :width]
    grad_o = lax.all_to_all(turned, ("chip", "core"), split_axis=2, concat_axis=1, tiled=True)
    grad_o = grad_o.transpose(0, 2, 1).astype(F32)
    grad_q = shared[..., q_wide : 2 * q_wide].reshape(layers, shard_rows, team * q_wide)
    grad_q = grad_q[..., :width].astype(F32)
    kv_parts = shared[..., 2 * q_wide :].astype(F32)
    kv_parts = kv_parts.reshape(layers, shard_rows, team, 2, SLOTS, HEAD)
    kv_heads = []
    for head in range(KV_HEADS):
        terms = [
            kv_parts[:, :, k, :, slot]
            for k in range(team)
            for slot in range(SLOTS)
            if (k * heads_here) // GROUP + slot == head
        ]
        kv_heads.append(sum(terms[1:], terms[0]))
    grad_kv = jnp.stack(kv_heads, axis=3).reshape(layers, shard_rows, 2 * kv_half)
    grad_bc = jnp.stack([jnp.sum(parts[4].astype(F32), axis=0) for parts in sums])[..., : 2 * STATE]

    def halves(which, begin, end):
        return [
            jnp.stack(by_core(*(part[:, begin:end] for part in parts[which]))).astype(F32)
            for parts in sums
        ]

    grad_in = jnp.stack(
        [
            pair.reshape(CORES, shard_rows, 3, wide)[..., :channels]
            .transpose(1, 2, 0, 3)
            .reshape(shard_rows, 3, CORES * channels)
            for pair in halves(2, 0, 3 * wide)
        ]
    )
    grad_out = jnp.stack(
        [
            pair.transpose(0, 2, 1).reshape(CORES * channels, shard_rows)
            for pair in halves(1, 0, channels)
        ]
    )
    grad_gu = jnp.stack(
        [
            pair.reshape(CORES, shard_rows, 2, hidden_here)
            .transpose(1, 2, 0, 3)
            .reshape(shard_rows, 2, CORES * hidden_here)
            for pair in halves(0, 0, 2 * hidden_here)
        ]
    )
    grad_down = jnp.stack(
        [
            pair.transpose(0, 2, 1).reshape(CORES * hidden_here, shard_rows)
            for pair in halves(0, 2 * hidden_here, 3 * hidden_here)
        ]
    )
    small = jnp.sum(lax.all_gather(jnp.stack([parts[5] for parts in sums]), "chip"), axis=0)
    small = share_columns(small, swap_cores(small))
    place = chip * CORES + core
    gain_full = jnp.sum(small[..., : 4 * width], axis=0).reshape(layers, 4, width)
    grad_gains = lax.dynamic_slice_in_dim(gain_full, place * shard_rows, shard_rows, 2)
    ssm_full = small[..., 4 * width :].reshape(team, layers, 3, channels)
    ssm_full = ssm_full.transpose(1, 2, 0, 3).reshape(layers, 3, team * channels)
    share = team * channels // (chips * CORES)
    ssm_own = lax.dynamic_slice_in_dim(ssm_full, place * share, share, 2)
    return (
        block_out, grad_stream, grad_q, grad_kv, grad_o, grad_in,
        ssm_own[:, 0], ssm_own[:, 1], ssm_own[:, 2], grad_bc, grad_out, grad_gains, grad_gu, grad_down,
    )


def solution(mesh):
    fsdp, tp = mesh.shape["fsdp"], mesh.shape["tp"]
    inner = Mesh(mesh.devices.reshape(fsdp // CORES, CORES, tp), ("chip", "core", "tp"))
    shards = ("chip", "core")
    tokens = P(("chip", "core", "tp"), None)
    by_row = P(None, shards, None)
    return jax.shard_map(
        body,
        mesh=inner,
        in_specs=(
            tokens, P(), by_row, by_row, by_row, P(None, shards, None, "tp"),
            P(None, "tp"), P(None, "tp"), P(None, "tp"), P(), P(None, "tp", shards), P(),
            P(None, shards, None, "tp"), P(None, "tp", shards), tokens,
        ),
        out_specs=(
            tokens, tokens, by_row, by_row, by_row, P(None, shards, None, "tp"),
            P(None, shards), P(None, shards), P(None, shards), by_row, P(None, "tp", shards),
            P(None, None, shards), P(None, shards, None, "tp"), P(None, "tp", shards),
        ),
        check_vma=False,
    )
```

time: 2970 us -> 2010 us (0.68)
  waiting for transfers between devices: 1320 us -> 613 us
  other arithmetic: 485 us -> 172 us
  matrix products: 522 us -> 234 us
  Pallas kernels: 0 us -> 248 us
  starting transfers between devices: 18.5 us -> 156 us
  blocking collectives: 151 us -> 42.1 us
  local copies, waits for them, and re-layouts: 424 us -> 511 us
    unnamed x69 -> x16, waiting for transfers between devices: 725 us -> 0.2 us
    ppermute x8 -> x122, waiting for transfers between devices: 52.8 us -> 536 us  [the longest x81 519 us: from_peer(): lax.ppermute(value, 'tp', [(n, n ^ k) for n in range(lax.axis_size('tp'))])]
    all_gather x22 -> x6, waiting for transfers between devices: 419 us -> 72.3 us  [own_halves(): return lax.all_gather(pair, 'chip', axis=0, tiled=True)]
    dot_general x264 -> x40, matrix products: 522 us -> 234 us  [the longest x14 93.8 us: dot(): return jnp.dot(a, b, preferred_element_type=F32).astype(out)]
    reduce_sum x60 -> x4, other arithmetic: 275 us -> 0.99 us  [the longest x2 0.76 us: body(): jnp.sum(parts[4].astype(F32), axis=0)]
    pallas_call x0 -> x12, Pallas kernels: none -> 248 us  [the longest x2 89 us: back(): self.call(scan_back_kernel, [self.tall(0), self.tall(0), self.tall(1), se...]
    ppermute x8 -> x122, starting transfers between devices: 14.4 us -> 150 us  [the longest x81 134 us: from_peer(): lax.ppermute(value, 'tp', [(n, n ^ k) for n in range(lax.axis_size('tp'))])]
    psum x1 -> x0, waiting for transfers between devices: 119 us -> none  [reduce_grads(): lax.psum(shards[0].astype(jnp.bfloat16), 'tp').astype(jnp.float32)]
  transfers between devices with their start and end apart: 54 -> 135, of which waited for: 32 -> 54; matrix products, arithmetic and copies ran while one was open for 33% -> 41% of each run, Pallas kernels for 0% -> 12%
where the time goes in v1:
time: 2010 us; the launch traced here: 2000 us
  waiting for transfers between devices  613 us (30%)
  local copies, waits for them, and re-layouts  511 us (25%)
  Pallas kernels  248 us (12%)
  matrix products  234 us (12%)
  other arithmetic  172 us (9%)
  starting transfers between devices  156 us (8%)
  blocking collectives  42.1 us (2%)
  between operations  23.3 us (1%)
    ppermute x81, waiting for transfers between devices, from_peer(): lax.ppermute(value, 'tp', [(n, n ^ k) for n in range(lax.axis_size('tp'))])  519 us
    ppermute x81, starting transfers between devices, from_peer(): lax.ppermute(value, 'tp', [(n, n ^ k) for n in range(lax.axis_size('tp'))])  134 us
    unnamed x501, local copies, waits for them, and re-layouts  126 us
    dot_general x14, matrix products, dot(): return jnp.dot(a, b, preferred_element_type=F32).astype(out)  93.8 us
    pallas_call x2, Pallas kernels, back(): self.call(scan_back_kernel, [self.tall(0), self.tall(0), self.tall(1), se...  89 us
    dot_general x14, matrix products, dot_nt(): lax.dot_general(a, b, (((1,), (1,)), ((), ())), preferred_element_type=F32)  85 us
    all_gather x6, waiting for transfers between devices, own_halves(): return lax.all_gather(pair, 'chip', axis=0, tiled=True)  72.3 us
    dot_general x12, matrix products, dot_tn(): lax.dot_general(a, b, (((0,), (0,)), ((), ())), preferred_element_type=F32)  55.3 us
  transfers between devices with their start and end apart: 135, of which 54 were waited for; matrix products, arithmetic and copies ran while one was open for 41% of the time, Pallas kernels for 12%

profile of v1, /device:TPU:0, one launch (start us, length us, event | category | flops | bytes accessed | tf_op | source)
XLA Modules:
  0.0 1999.5 jit_solution(853268544630274609)
XLA Ops:
  26.4 72.2 %all-gather.13.cloned.1.call-done = bf16[1600,2048]{1,0:T(8,128)(2,1)} async-done(((bf16[400,2048]{1,0:T(8,128)(2,1)}), bf16[1600,2048]{1,0:T(8,128)(2,1)}) %all-gather.13.cloned.1.call-update) | async-done | bytes 6553616 | tf_op jit(solution)/shard_map/all_gather | solution.py:671
  207.1 16.7 shard_map.254
  254.1 18.0 shard_map.256
  339.3 20.8 %collective-permute-done.14 = bf16[128,1600]{1,0:T(8,128)(2,1)S(1)} collective-permute-done((bf16[128,1600]{1,0:T(8,128)(2,1)S(1)}, bf16[128,1600]{1,0:T(8,128)(2,1)S(1)}, u32[]{:S(2)}, u32[]{:S(2)}) %collective-permute-start.14) | collective-permute-done | bytes 409632 | tf_op jit(solution)/shard_map/ppermute | solution.py:608
  397.1 22.0 %collective-permute-done.17 = bf16[128,1600]{1,0:T(8,128)(2,1)S(1)} collective-permute-done((bf16[128,1600]{1,0:T(8,128)(2,1)S(1)}, bf16[128,1600]{1,0:T(8,128)(2,1)S(1)}, u32[]{:S(2)}, u32[]{:S(2)}) %collective-permute-start.17) | collective-permute-done | bytes 409632 | tf_op jit(solution)/shard_map/ppermute | solution.py:608
  492.0 15.1 collective-permute-done.24
  507.1 23.6 %collective-permute-done.23 = bf16[128,1600]{1,0:T(8,128)(2,1)S(1)} collective-permute-done((bf16[128,1600]{1,0:T(8,128)(2,1)S(1)}, bf16[128,1600]{1,0:T(8,128)(2,1)S(1)}, u32[]{:S(2)}, u32[]{:S(2)}) %collective-permute-start.23) | collective-permute-done | bytes 409632 | tf_op jit(solution)/shard_map/ppermute | solution.py:608
  546.9 16.0 collective-permute-start.50
  609.2 11.0 fusion.8
  628.4 16.3 shard_map.257
  669.4 17.9 shard_map.259
  730.9 11.5 collective-permute-done.33
  750.6 18.5 collective-permute-done.39
  786.2 21.6 %collective-permute-done.42 = bf16[128,1600]{1,0:T(8,128)(2,1)S(1)} collective-permute-done((bf16[128,1600]{1,0:T(8,128)(2,1)S(1)}, bf16[128,1600]{1,0:T(8,128)(2,1)S(1)}, u32[]{:S(2)}, u32[]{:S(2)}) %collective-permute-start.42) | collective-permute-done | bytes 409632 | tf_op jit(solution)/shard_map/ppermute | solution.py:608
  921.1 22.3 %collective-permute-done.56 = bf16[128,1600]{1,0:T(8,128)(2,1)S(1)} collective-permute-done((bf16[128,1600]{1,0:T(8,128)(2,1)S(1)}, bf16[128,1600]{1,0:T(8,128)(2,1)S(1)}, u32[]{:S(2)}, u32[]{:S(2)}) %collective-permute-start.56) | collective-permute-done | bytes 409632 | tf_op jit(solution)/shard_map/ppermute | solution.py:608
  945.6 24.8 %collective-permute-done.48 = bf16[128,1600]{1,0:T(8,128)(2,1)S(1)} collective-permute-done((bf16[128,1600]{1,0:T(8,128)(2,1)S(1)}, bf16[128,1600]{1,0:T(8,128)(2,1)S(1)}, u32[]{:S(2)}, u32[]{:S(2)}) %collective-permute-start.48) | collective-permute-done | bytes 409632 | tf_op jit(solution)/shard_map/ppermute | solution.py:608
  989.0 20.8 %collective-permute-done.59 = bf16[128,512]{1,0:T(8,128)(2,1)S(1)} collective-permute-done((bf16[128,512]{1,0:T(8,128)(2,1)S(1)}, bf16[128,512]{1,0:T(8,128)(2,1)S(1)}, u32[]{:S(2)}, u32[]{:S(2)}) %collective-permute-start.59) | collective-permute-done | bytes 131104 | tf_op jit(solution)/shard_map/ppermute | solution.py:608
  1016.0 25.3 %shard_map.260 = (bf16[1024,512]{1,0:T(8,128)(2,1)}, bf16[1024,256]{1,0:T(8,128)(2,1)}, f32[1024,256]{1,0:T(8,128)}) custom-call(s32[1]{0:T(128)} %bitcast.me_ref, bf16[1024,512]{1,0:T(8,128)(2,1)} %copy.805.q_ref, bf16[1024,256]{1,0:T(8,128)(2,1)} %copy-done.174, bf16[1024,256]{1,0:T(8,128)(2,1)} %copy-done.79, s32[1024,1]{1,0:T(8,128)} %maximum_subtract_fusion.refs_2_, ...), custom_call_target="tpu_custom_call" | custom-call | flops 15000000512 | bytes 12000000 | tf_op jit(solution)/shard_map/pallas_call | solution.py:588
  1053.8 12.0 collective-permute-done.64
  1148.5 44.6 %shard_map.262 = (bf16[1024,512]{1,0:T(8,128)(2,1)}, bf16[1024,512]{1,0:T(8,128)(2,1)}, bf16[1024,512]{1,0:T(8,128)(2,1)}, bf16[1024,128]{1,0:T(8,128)(2,1)}, f32[8,512]{1,0:T(8,128)}) custom-call(s32[1]{0:T(128)} %bitcast.me_ref, f32[1024,512]{1,0:T(8,128)} %fusion.84.grad_ref, f32[1024,1664]{1,0:T(8,128)} %pad_maximum_fusion.3.u_ref.pre_ref.bc_ref.gate_ref, ...), custom_call_target="tpu_custom_call" | custom-call | flops 20000000000 | bytes 15728640 | tf_op jit(solution)/shard_map/pallas_call | solution.py:456
  1259.5 14.3 collective-permute-done.69
  1289.2 22.5 %collective-permute-done.72 = bf16[128,1600]{1,0:T(8,128)(2,1)S(1)} collective-permute-done((bf16[128,1600]{1,0:T(8,128)(2,1)S(1)}, bf16[128,1600]{1,0:T(8,128)(2,1)S(1)}, u32[]{:S(2)}, u32[]{:S(2)}) %collective-permute-start.72) | collective-permute-done | bytes 409632 | tf_op jit(solution)/shard_map/ppermute | solution.py:608
  1369.5 11.7 collective-permute-done.78
  1381.3 11.6 collective-permute-done.77
  1410.9 20.2 %collective-permute-done.80 = bf16[128,512]{1,0:T(8,128)(2,1)S(1)} collective-permute-done((bf16[128,512]{1,0:T(8,128)(2,1)S(1)}, bf16[128,512]{1,0:T(8,128)(2,1)S(1)}, u32[]{:S(2)}, u32[]{:S(2)}) %collective-permute-start.80) | collective-permute-done | bytes 131104 | tf_op jit(solution)/shard_map/ppermute | solution.py:608
  1437.1 25.1 %shard_map.263 = (bf16[1024,512]{1,0:T(8,128)(2,1)}, bf16[1024,256]{1,0:T(8,128)(2,1)}, f32[1024,256]{1,0:T(8,128)}) custom-call(s32[1]{0:T(128)} %bitcast.me_ref, bf16[1024,512]{1,0:T(8,128)(2,1)} %copy.803.q_ref, bf16[1024,256]{1,0:T(8,128)(2,1)} %collective-permute-done.5.refs_0_, bf16[1024,256]{1,0:T(8,128)(2,1)} %get-tuple-element.328.refs_1_, ...), custom_call_target="tpu_custom_call" | custom-call | flops 15000000512 | bytes 12000000 | tf_op jit(solution)/shard_map/pallas_call | solution.py:588
  1474.5 12.8 collective-permute-done.85
  1570.9 44.4 %shard_map.265 = (bf16[1024,512]{1,0:T(8,128)(2,1)}, bf16[1024,512]{1,0:T(8,128)(2,1)}, bf16[1024,512]{1,0:T(8,128)(2,1)}, bf16[1024,128]{1,0:T(8,128)(2,1)}, f32[8,512]{1,0:T(8,128)}) custom-call(s32[1]{0:T(128)} %bitcast.me_ref, f32[1024,512]{1,0:T(8,128)} %fusion.89.grad_ref, f32[1024,1664]{1,0:T(8,128)} %pad_maximum_fusion.1.u_ref.pre_ref.bc_ref.gate_ref, ...), custom_call_target="tpu_custom_call" | custom-call | flops 20000000000 | bytes 15728640 | tf_op jit(solution)/shard_map/pallas_call | solution.py:456
  1675.5 28.6 %collective-permute-done.106 = bf16[2,200,768]{2,1,0:T(8,128)(2,1)} collective-permute-done((bf16[2,200,768]{2,1,0:T(8,128)(2,1)}, bf16[2,200,768]{2,1,0:T(8,128)(2,1)}, u32[]{:S(2)}, u32[]{:S(2)}) %collective-permute-start.106) | collective-permute-done | bytes 614432 | tf_op jit(solution)/shard_map/ppermute | solution.py:608
  1758.9 11.3 collective-permute-done.90
  1854.9 35.2 %collective-permute-done.98 = bf16[2,200,768]{2,1,0:T(8,128)(2,1)} collective-permute-done((bf16[2,200,768]{2,1,0:T(8,128)(2,1)}, bf16[2,200,768]{2,1,0:T(8,128)(2,1)}, u32[]{:S(2)}, u32[]{:S(2)}) %collective-permute-start.98) | collective-permute-done | bytes 614432 | tf_op jit(solution)/shard_map/ppermute | solution.py:608
  1902.5 11.1 copy.767
  (1276 shorter events, 1276.2 us)
Async XLA Ops:
  7.2 91.5 %all-gather.13.cloned.1.call-start = ((), (), s32[]{:S(2)}) async-start(), calls=%async_computation.7 | async-start | bytes 8192000 | tf_op jit(solution)/shard_map/all_gather | solution.py:671
  23.6 250.8 %all-gather.15.cloned.1.call-start = ((), (), s32[]{:S(2)}) async-start(), calls=%async_computation.8 | async-start | bytes 5632000 | tf_op jit(solution)/shard_map/all_gather | solution.py:671
  107.5 327.5 %all-gather.17.cloned.1.call-start = ((), (), s32[]{:S(2)}) async-start(), calls=%async_computation.9 | async-start | bytes 8704000 | tf_op jit(solution)/shard_map/all_gather | solution.py:671
  139.8 398.2 %all-gather.21.cloned.1.call-start = ((), (), s32[]{:S(2)}) async-start(), calls=%async_computation.11 | async-start | bytes 5632000 | tf_op jit(solution)/shard_map/all_gather | solution.py:671
  179.8 92.3 %collective-permute-start.35 = (bf16[200,1408]{1,0:T(8,128)(2,1)}, bf16[200,1408]{1,0:T(8,128)(2,1)}, u32[]{:S(2)}, u32[]{:S(2)}) collective-permute-start(bf16[200,1408]{1,0:T(8,128)(2,1)} %bitcast.469), channel_id=1, source_target_pairs={{0,4},{4,0},{1,5},{5,1},{2,6},{6,2},{3,7},{7,3},{8,12},{12,8},{9,1... | collective-permute-start | bytes 1689608 | tf_op jit(solution)/shard_map/ppermute | solution.py:604
  274.4 326.7 %all-gather.19.cloned.1.call-start = ((), (), s32[]{:S(2)}) async-start(), calls=%async_computation.10 | async-start | bytes 8192000 | tf_op jit(solution)/shard_map/all_gather | solution.py:671
  301.0 60.0 %collective-permute-start.11 = (bf16[2048,800]{0,1:T(8,128)(2,1)}, bf16[2048,800]{0,1:T(8,128)(2,1)}, u32[]{:S(2)}, u32[]{:S(2)}) collective-permute-start(bf16[2048,800]{0,1:T(8,128)(2,1)} %copy.634), channel_id=1, source_target_pairs={{0,4},{4,0},{1,5},{5,1},{2,6},{6,2},{3,7},{7,3},{8,12},{12,8},{9,1... | collective-permute-start | bytes 9830408 | tf_op jit(solution)/shard_map/ppermute | solution.py:604
  307.7 67.4 %collective-permute-start.7 = (bf16[128,512]{0,1:T(8,128)(2,1)S(1)}, bf16[128,512]{0,1:T(8,128)(2,1)}, u32[]{:S(2)}, u32[]{:S(2)}) collective-permute-start(bf16[128,512]{0,1:T(8,128)(2,1)S(1)} %get-tuple-element.368), channel_id=1, source_target_pairs={{0,1},{1,0},{2,3},{3,2},{4,5},{5,4},{6,7},{7,6},{8,9},{9,8},{10,11... | collective-permute-start | bytes 393224 | tf_op jit(solution)/shard_map/ppermute | solution.py:608
  389.7 444.1 %all-gather.23.cloned.1.call-start = ((), (), s32[]{:S(2)}) async-start(), calls=%async_computation.12 | async-start | bytes 8704000 | tf_op jit(solution)/shard_map/all_gather | solution.py:671
  458.1 237.4 %collective-permute-start.52 = (bf16[128,1600]{0,1:T(8,128)(2,1)}, bf16[128,1600]{0,1:T(8,128)(2,1)}, u32[]{:S(2)}, u32[]{:S(2)}) collective-permute-start(bf16[128,1600]{0,1:T(8,128)(2,1)} %param.29), channel_id=1, source_target_pairs={{0,3},{1,2},{2,1},{3,0},{4,7},{5,6},{6,5},{7,4},{8,11},{9,10},{10,... | collective-permute-start | bytes 1228808 | tf_op jit(solution)/shard_map/ppermute | solution.py:608
  459.5 236.0 %collective-permute-start.51 = (bf16[128,1600]{0,1:T(8,128)(2,1)}, bf16[128,1600]{0,1:T(8,128)(2,1)}, u32[]{:S(2)}, u32[]{:S(2)}) collective-permute-start(bf16[128,1600]{0,1:T(8,128)(2,1)} %param.29), channel_id=1, source_target_pairs={{0,2},{1,3},{2,0},{3,1},{4,6},{5,7},{6,4},{7,5},{8,10},{9,11},{10,... | collective-permute-start | bytes 1228808 | tf_op jit(solution)/shard_map/ppermute | solution.py:608
  537.9 1006.6 %reduce-scatter.17.cloned.1.call-start = ((), (), s32[]{:S(2)}) async-start(), calls=%async_computation.14 | async-start | bytes 5120000 | tf_op jit(solution)/shard_map/reduce_scatter | solution.py:675
  546.9 148.6 %collective-permute-start.50 = (bf16[128,1600]{0,1:T(8,128)(2,1)}, bf16[128,1600]{0,1:T(8,128)(2,1)}, u32[]{:S(2)}, u32[]{:S(2)}) collective-permute-start(bf16[128,1600]{0,1:T(8,128)(2,1)} %param.29), channel_id=1, source_target_pairs={{0,1},{1,0},{2,3},{3,2},{4,5},{5,4},{6,7},{7,6},{8,9},{9,8},{10,11... | collective-permute-start | bytes 1228808 | tf_op jit(solution)/shard_map/ppermute | solution.py:608
  587.4 111.3 %collective-permute-start.36 = (bf16[2048,800]{0,1:T(8,128)(2,1)}, bf16[2048,800]{0,1:T(8,128)(2,1)}, u32[]{:S(2)}, u32[]{:S(2)}) collective-permute-start(bf16[2048,800]{0,1:T(8,128)(2,1)} %copy.666), channel_id=1, source_target_pairs={{0,4},{4,0},{1,5},{5,1},{2,6},{6,2},{3,7},{7,3},{8,12},{12,8},{9,1... | collective-permute-start | bytes 9830408 | tf_op jit(solution)/shard_map/ppermute | solution.py:604
  698.3 120.1 %collective-permute-start.53 = (bf16[512,1600]{0,1:T(8,128)(2,1)}, bf16[512,1600]{0,1:T(8,128)(2,1)}, u32[]{:S(2)}, u32[]{:S(2)}) collective-permute-start(bf16[512,1600]{0,1:T(8,128)(2,1)} %pad_maximum_fusion.29), channel_id=1, source_target_pairs={{0,4},{4,0},{1,5},{5,1},{2,6},{6,2},{3,7},{7,3},{8,12},{12,8},{9,1... | collective-permute-start | bytes 4915208 | tf_op jit(solution)/shard_map/ppermute | solution.py:604
  909.5 60.9 %collective-permute-start.48 = (bf16[128,1600]{1,0:T(8,128)(2,1)S(1)}, bf16[128,1600]{1,0:T(8,128)(2,1)S(1)}, u32[]{:S(2)}, u32[]{:S(2)}) collective-permute-start(bf16[128,1600]{1,0:T(8,128)(2,1)S(1)} %get-tuple-element.286), channel_id=1, source_target_pairs={{0,2},{1,3},{2,0},{3,1},{4,6},{5,7},{6,4},{7,5},{8,10},{9,11},{10,... | collective-permute-start | bytes 1228808 | tf_op jit(solution)/shard_map/ppermute | solution.py:608
  984.5 60.6 %collective-permute-start.102 = (bf16[128,1600]{1,0:T(8,128)(2,1)S(1)}, bf16[128,1600]{1,0:T(8,128)(2,1)}, u32[]{:S(2)}, u32[]{:S(2)}) collective-permute-start(bf16[128,1600]{1,0:T(8,128)(2,1)S(1)} %get-tuple-element.200), channel_id=1, source_target_pairs={{0,3},{1,2},{2,1},{3,0},{4,7},{5,6},{6,5},{7,4},{8,11},{9,10},{10,... | collective-permute-start | bytes 1228808 | tf_op jit(solution)/shard_map/ppermute | solution.py:608
  985.9 62.9 %collective-permute-start.101 = (bf16[128,1600]{1,0:T(8,128)(2,1)S(1)}, bf16[128,1600]{1,0:T(8,128)(2,1)}, u32[]{:S(2)}, u32[]{:S(2)}) collective-permute-start(bf16[128,1600]{1,0:T(8,128)(2,1)S(1)} %get-tuple-element.200), channel_id=1, source_target_pairs={{0,2},{1,3},{2,0},{3,1},{4,6},{5,7},{6,4},{7,5},{8,10},{9,11},{10,... | collective-permute-start | bytes 1228808 | tf_op jit(solution)/shard_map/ppermute | solution.py:608
  988.4 61.7 %collective-permute-start.100 = (bf16[128,1600]{1,0:T(8,128)(2,1)S(1)}, bf16[128,1600]{1,0:T(8,128)(2,1)}, u32[]{:S(2)}, u32[]{:S(2)}) collective-permute-start(bf16[128,1600]{1,0:T(8,128)(2,1)S(1)} %get-tuple-element.200), channel_id=1, source_target_pairs={{0,1},{1,0},{2,3},{3,2},{4,5},{5,4},{6,7},{7,6},{8,9},{9,8},{10,11... | collective-permute-start | bytes 1228808 | tf_op jit(solution)/shard_map/ppermute | solution.py:608
  1097.7 643.1 %reduce-scatter.25.cloned.1.call-start = ((), (), s32[]{:S(2)}) async-start(), calls=%async_computation.18 | async-start | bytes 8704000
  1124.8 676.0 %reduce-scatter.21.cloned.1.call-start = ((), (), s32[]{:S(2)}) async-start(), calls=%async_computation.16 | async-start | bytes 6656000
  1367.0 462.0 %reduce-scatter.15.cloned.1.call-start = ((), (), s32[]{:S(2)}) async-start(), calls=%async_computation.13 | async-start | bytes 5120000 | tf_op jit(solution)/shard_map/reduce_scatter | solution.py:675
  1406.5 57.8 %collective-permute-start.94 = (bf16[128,1600]{1,0:T(8,128)(2,1)S(1)}, bf16[128,1600]{1,0:T(8,128)(2,1)S(1)}, u32[]{:S(2)}, u32[]{:S(2)}) collective-permute-start(bf16[128,1600]{1,0:T(8,128)(2,1)S(1)} %get-tuple-element.198), channel_id=1, source_target_pairs={{0,3},{1,2},{2,1},{3,0},{4,7},{5,6},{6,5},{7,4},{8,11},{9,10},{10,... | collective-permute-start | bytes 1228808 | tf_op jit(solution)/shard_map/ppermute | solution.py:608
  1408.6 60.5 %collective-permute-start.93 = (bf16[128,1600]{1,0:T(8,128)(2,1)S(1)}, bf16[128,1600]{1,0:T(8,128)(2,1)}, u32[]{:S(2)}, u32[]{:S(2)}) collective-permute-start(bf16[128,1600]{1,0:T(8,128)(2,1)S(1)} %get-tuple-element.198), channel_id=1, source_target_pairs={{0,2},{1,3},{2,0},{3,1},{4,6},{5,7},{6,4},{7,5},{8,10},{9,11},{10,... | collective-permute-start | bytes 1228808 | tf_op jit(solution)/shard_map/ppermute | solution.py:608
  1410.1 60.3 %collective-permute-start.92 = (bf16[128,1600]{1,0:T(8,128)(2,1)S(1)}, bf16[128,1600]{1,0:T(8,128)(2,1)}, u32[]{:S(2)}, u32[]{:S(2)}) collective-permute-start(bf16[128,1600]{1,0:T(8,128)(2,1)S(1)} %get-tuple-element.198), channel_id=1, source_target_pairs={{0,1},{1,0},{2,3},{3,2},{4,5},{5,4},{6,7},{7,6},{8,9},{9,8},{10,11... | collective-permute-start | bytes 1228808 | tf_op jit(solution)/shard_map/ppermute | solution.py:608
  1516.1 411.7 %reduce-scatter.23.cloned.1.call-start = ((), (), s32[]{:S(2)}) async-start(), calls=%async_computation.17 | async-start | bytes 8704000
  1541.6 412.9 %reduce-scatter.19.cloned.1.call-start = ((), (), s32[]{:S(2)}) async-start(), calls=%async_computation.15 | async-start | bytes 6656000
  1545.7 103.5 %collective-permute-start.104 = (bf16[200,1280]{1,0:T(8,128)(2,1)S(1)}, bf16[200,1280]{1,0:T(8,128)(2,1)S(1)}, u32[]{:S(2)}, u32[]{:S(2)}) collective-permute-start(bf16[200,1280]{1,0:T(8,128)(2,1)S(1)} %get-tuple-element.332), channel_id=1, source_target_pairs={{0,4},{4,0},{1,5},{5,1},{2,6},{6,2},{3,7},{7,3},{8,12},{12,8},{9,1... | collective-permute-start | bytes 1536008 | tf_op jit(solution)/shard_map/ppermute | solution.py:604
  1664.2 62.2 %collective-permute-start.88 = (bf16[512,1600]{0,1:T(8,128)(2,1)}, bf16[512,1600]{0,1:T(8,128)(2,1)}, u32[]{:S(2)}, u32[]{:S(2)}) collective-permute-start(bf16[512,1600]{0,1:T(8,128)(2,1)} %copy.727), channel_id=1, source_target_pairs={{0,4},{4,0},{1,5},{5,1},{2,6},{6,2},{3,7},{7,3},{8,12},{12,8},{9,1... | collective-permute-start | bytes 4915208 | tf_op jit(solution)/shard_map/ppermute | solution.py:604
  1743.2 60.4 %collective-permute-start.121 = (bf16[200,2176]{1,0:T(8,128)(2,1)}, bf16[200,2176]{1,0:T(8,128)(2,1)}, u32[]{:S(2)}, u32[]{:S(2)}) collective-permute-start(bf16[200,2176]{1,0:T(8,128)(2,1)} %get-tuple-element.271), channel_id=1, source_target_pairs={{0,4},{4,0},{1,5},{5,1},{2,6},{6,2},{3,7},{7,3},{8,12},{12,8},{9,1... | collective-permute-start | bytes 2611208 | tf_op jit(solution)/shard_map/ppermute | solution.py:604
  1836.3 53.8 %collective-permute-start.98 = (bf16[2,200,768]{2,1,0:T(8,128)(2,1)}, bf16[2,200,768]{2,1,0:T(8,128)(2,1)}, u32[]{:S(2)}, u32[]{:S(2)}) collective-permute-start(bf16[2,200,768]{2,1,0:T(8,128)(2,1)} %copy.736), channel_id=1, source_target_pairs={{0,2},{1,3},{2,0},{3,1},{4,6},{5,7},{6,4},{7,5},{8,10},{9,11},{10,... | collective-permute-start | bytes 1843208 | tf_op jit(solution)/shard_map/ppermute | solution.py:608
  1836.3 56.0 %collective-permute-start.97 = (bf16[2,200,768]{2,1,0:T(8,128)(2,1)}, bf16[2,200,768]{2,1,0:T(8,128)(2,1)}, u32[]{:S(2)}, u32[]{:S(2)}) collective-permute-start(bf16[2,200,768]{2,1,0:T(8,128)(2,1)} %copy.736), channel_id=1, source_target_pairs={{0,1},{1,0},{2,3},{3,2},{4,5},{5,4},{6,7},{7,6},{8,9},{9,8},{10,11... | collective-permute-start | bytes 1843208 | tf_op jit(solution)/shard_map/ppermute | solution.py:608
  (298 other events, 4744.4 us)
Sparse Core Ops, SparseCore 0:
  23.7 74.9 all-gather.12
  107.6 55.2 all-gather.14
  165.4 81.5 all-gather.16
  274.5 55.2 all-gather.20
  389.8 71.7 all-gather.18
  538.0 75.9 all-gather.22
  1097.8 50.8 reduce-scatter.16
  1151.7 78.3 reduce-scatter.24
  1367.2 62.3 reduce-scatter.20
  1516.2 50.6 reduce-scatter.14
  1570.0 78.0 reduce-scatter.22
  1664.3 63.2 reduce-scatter.18
